TPU v7x, 32 devices: a whole 2x2x4 slice. The times are simulated.
32 devices in a mesh: section: 4 (over y, x), dp: 8 (over z, core).
Axes of the slice: x: 2, y: 2, z: 4, core: 2. Of those that a mesh axis runs over, the one named last changes fastest.
Arguments:
- features: bfloat16 [32, 16, 16, 256], P('dp', 'section'), may hold values from -6 to 6
- tower_class: float32 [4, 2304, 256], P('section', 'dp'), may hold values from -0.125 to 0.125
- bias_class: float32 [4, 256], replicated, may hold values from -3 to 3
- tower_boxes: float32 [4, 2304, 256], P('section', 'dp'), may hold values from -0.125 to 0.125
- bias_boxes: float32 [4, 256], replicated, may hold values from -3 to 3
- head_class: float32 [2304, 720], P('dp', 'section'), may hold values from -0.125 to 0.125
- head_class_bias: float32 [720], replicated, may hold values from -4.6 to -3
- head_boxes: float32 [2304, 36], P('dp', 'section'), may hold values from -0.125 to 0.125
- head_boxes_bias: float32 [36], replicated, may hold values from -3 to 3
- anchor_state: int32 [32, 16, 144], P('dp'), may hold values from 0 to 2, as said below
- class_labels: int32 [32, 16, 144], P('dp'), may hold values from 0 to 79
- box_targets: float32 [32, 16, 576], P('dp'), may hold values from -6 to 6
- valid_rows: int32 [32], P('dp'), may hold values from 4 to 16
Outputs:
- grad_features: bfloat16 [32, 16, 16, 256], P('dp', 'section')
- grad_tower_class: float32 [4, 2304, 256], P('section', 'dp')
- grad_bias_class: float32 [4, 256], replicated
- grad_tower_boxes: float32 [4, 2304, 256], P('section', 'dp')
- grad_bias_boxes: float32 [4, 256], replicated
- grad_head_class: float32 [2304, 720], P('dp', 'section')
- grad_head_class_bias: float32 [720], replicated
- grad_head_boxes: float32 [2304, 36], P('dp', 'section')
- grad_head_boxes_bias: float32 [36], replicated
Inputs may be any that keep to these rules, and one draw needn't show every extreme that they name: `anchor_state`: 0 marks a negative anchor, 1 a positive one, 2 an ignored one.
All inputs are finite; a program needn't handle non-finite values.
Results may differ from a plain program's by a relative error of at most 0.018.
Values may be sent and summed in bfloat16 or wider, within the bound.
A program may use at most 256 MiB of HBM per device.

v0:
```python
import jax
import jax.numpy as jnp
from jax import lax
from jax.sharding import PartitionSpec as P

K = 80
A = 9
LAYERS = 4
TILE = 16
MICRO = 4


huber_beta = 1.0 / 9.0


def shifted(block, axis, distance):
    devices = range(lax.axis_size(axis))
    route = [(i - distance, i) for i in devices if i - distance in devices]
    return lax.ppermute(block, axis, route)


def anchor_masks(anchor_state, valid_rows):
    tile_count = anchor_state.shape[0]
    anchor_kind = anchor_state.reshape(tile_count, TILE, TILE, A)
    row_index = lax.broadcasted_iota(jnp.int32, (tile_count, TILE, 1, 1), 1)
    inside = row_index < valid_rows.reshape(tile_count, 1, 1, 1)
    positive = jnp.logical_and(anchor_kind == 1, inside).astype(jnp.float32)
    counted = jnp.logical_and(anchor_kind != 2, inside).astype(jnp.float32)
    return (positive, counted)


def head_loss(logits, box_values, positive, counted, class_labels, box_targets, normalizer):
    tile_count = logits.shape[0]
    scores = logits.reshape(tile_count, TILE, TILE, A, K)
    labels = class_labels.reshape(tile_count, TILE, TILE, A, 1)
    classes = lax.broadcasted_iota(jnp.int32, (1, 1, 1, 1, K), 4)
    target = (labels == classes).astype(jnp.float32) * positive[..., None]
    chance = jax.nn.sigmoid(scores)
    entropy = jax.nn.softplus(scores) - target * scores
    agreement = chance * target + (1.0 - chance) * (1.0 - target)
    balance = 0.25 * target + 0.75 * (1.0 - target)
    focal_terms = balance * (1.0 - agreement) ** 2 * entropy
    focal_sum = jnp.sum(focal_terms * counted[..., None])
    offsets = box_values.reshape(tile_count, TILE, TILE, A, 4) - box_targets.reshape(
        tile_count, TILE, TILE, A, 4
    )
    spread = jnp.abs(offsets)
    huber_terms = jnp.where(
        spread < huber_beta, 0.5 * offsets * offsets / huber_beta, spread - 0.5 * huber_beta
    )
    box_sum = jnp.sum(huber_terms * positive[..., None])
    return (focal_sum + box_sum) / normalizer


def unfold(values):
    tile_count, tile_side, channels = (values.shape[0], values.shape[1], values.shape[3])
    padded = jnp.pad(values, ((0, 0), (1, 1), (1, 1), (0, 0)))
    pieces = [
        padded[:, row_shift : row_shift + tile_side, col_shift : col_shift + tile_side, :]
        for row_shift in range(3)
        for col_shift in range(3)
    ]
    return jnp.concatenate(pieces, axis=-1).reshape(
        tile_count * tile_side * tile_side, 9 * channels
    )


def fold_back(columns, tile_count, tile_side, channels):
    shaped = columns.reshape(tile_count, tile_side, tile_side, 9 * channels)
    padded = jnp.zeros((tile_count, tile_side + 2, tile_side + 2, channels), jnp.float32)
    for tap_index in range(9):
        row_shift = tap_index // 3
        col_shift = tap_index % 3
        padded = padded.at[
            :, row_shift : row_shift + tile_side, col_shift : col_shift + tile_side, :
        ].add(shaped[..., tap_index * channels : (tap_index + 1) * channels])
    return padded[:, 1 : tile_side + 1, 1 : tile_side + 1, :]


def weight_grad(columns, upstream):
    return jnp.einsum("pk,pc->kc", columns, upstream, preferred_element_type=jnp.float32)


def input_cols(upstream, weight):
    return jnp.einsum("pc,kc->pk", upstream, weight, preferred_element_type=jnp.float32)


def pick(buffer, slot_index):
    return lax.dynamic_index_in_dim(buffer, slot_index, 0, keepdims=False)


def store(buffer, update, slot_index, active):
    return lax.dynamic_update_index_in_dim(
        buffer, jnp.where(active, update, pick(buffer, slot_index)), slot_index, 0
    )


def per_device(
    features,
    tower_class,
    bias_class,
    tower_boxes,
    bias_boxes,
    head_class,
    head_class_bias,
    head_boxes,
    head_boxes_bias,
    anchor_state,
    class_labels,
    box_targets,
    valid_rows,
):
    section_count = lax.axis_size("section")
    section_index = lax.axis_index("section")
    final_section = section_count - 1
    is_first = section_index == 0
    is_final = section_index == final_section
    tile_dev = features.shape[0]
    per_micro = tile_dev // MICRO
    whole = lax.all_gather(features, "section", axis=1, tiled=True)
    tile_side = whole.shape[1]
    channels = whole.shape[3]
    pixels = per_micro * tile_side * tile_side
    act_shape = (per_micro, tile_side, tile_side, channels)
    positive, counted = anchor_masks(anchor_state, valid_rows)
    found = lax.psum(jnp.sum(positive), "dp")
    normalizer = jnp.maximum(found, 1.0)
    gathered = (
        lax.all_gather(tower_class.astype(jnp.bfloat16), "dp", axis=1, tiled=True),
        lax.all_gather(tower_boxes.astype(jnp.bfloat16), "dp", axis=1, tiled=True),
        lax.all_gather(head_class.astype(jnp.bfloat16), "dp", axis=0, tiled=True),
        lax.all_gather(head_boxes.astype(jnp.bfloat16), "dp", axis=0, tiled=True),
    )
    weight_class = gathered[0][0]
    weight_boxes = gathered[1][0]
    head_weight_class, head_weight_boxes = (
        lax.all_gather(gathered[2], "section", axis=1, tiled=True),
        lax.all_gather(gathered[3], "section", axis=1, tiled=True),
    )
    layer_bias_class = lax.dynamic_index_in_dim(bias_class, section_index, 0, keepdims=False)
    layer_bias_boxes = lax.dynamic_index_in_dim(bias_boxes, section_index, 0, keepdims=False)
    class_width = head_weight_class.shape[1]
    boxes_width = head_weight_boxes.shape[1]
    patch_width = head_weight_class.shape[0]

    def head_pass(stored_class, stored_boxes, slot_index):
        cols_class = unfold(stored_class)
        cols_boxes = unfold(stored_boxes)
        logits = (
            jnp.dot(cols_class, head_weight_class, preferred_element_type=jnp.float32)
            + head_class_bias
        )
        box_values = (
            jnp.dot(cols_boxes, head_weight_boxes, preferred_element_type=jnp.float32)
            + head_boxes_bias
        )
        start = slot_index * per_micro
        pos_here = lax.dynamic_slice_in_dim(positive, start, per_micro, 0)
        counted_here = lax.dynamic_slice_in_dim(counted, start, per_micro, 0)
        labels_here = lax.dynamic_slice_in_dim(class_labels, start, per_micro, 0)
        targets_here = lax.dynamic_slice_in_dim(box_targets, start, per_micro, 0)

        def local_loss(logit_part, box_part):
            return head_loss(
                logit_part.reshape(per_micro, tile_side, tile_side, class_width),
                box_part.reshape(per_micro, tile_side, tile_side, boxes_width),
                pos_here,
                counted_here,
                labels_here,
                targets_here,
                normalizer,
            )

        total_loss, pullback = jax.vjp(local_loss, logits, box_values)
        grad_logits, grad_box = pullback(jnp.ones_like(total_loss))
        grad_logits = grad_logits.astype(jnp.bfloat16)
        grad_box = grad_box.astype(jnp.bfloat16)
        back_class = fold_back(
            input_cols(grad_logits, head_weight_class), per_micro, tile_side, channels
        )
        back_boxes = fold_back(
            input_cols(grad_box, head_weight_boxes), per_micro, tile_side, channels
        )
        return (
            weight_grad(cols_class, grad_logits),
            weight_grad(cols_boxes, grad_box),
            jnp.sum(grad_logits.astype(jnp.float32), 0),
            jnp.sum(grad_box.astype(jnp.float32), 0),
            back_class,
            back_boxes,
        )

    def head_spare(stored_class, stored_boxes, slot_index):
        return (
            jnp.zeros((patch_width, class_width), jnp.float32),
            jnp.zeros((patch_width, boxes_width), jnp.float32),
            jnp.zeros((class_width,), jnp.float32),
            jnp.zeros((boxes_width,), jnp.float32),
            jnp.zeros(act_shape, jnp.float32),
            jnp.zeros(act_shape, jnp.float32),
        )

    kept_class = jnp.zeros((MICRO,) + act_shape, jnp.bfloat16)
    kept_boxes = jnp.zeros((MICRO,) + act_shape, jnp.bfloat16)
    kept_pre_class = jnp.zeros((MICRO, pixels, channels), jnp.float32)
    kept_pre_boxes = jnp.zeros((MICRO, pixels, channels), jnp.float32)
    head_back_class = jnp.zeros((MICRO,) + act_shape, jnp.float32)
    head_back_boxes = jnp.zeros((MICRO,) + act_shape, jnp.float32)
    grad_head_class = jnp.zeros((patch_width, class_width), jnp.float32)
    grad_head_boxes = jnp.zeros((patch_width, boxes_width), jnp.float32)
    grad_hbias_class = jnp.zeros((class_width,), jnp.float32)
    grad_hbias_boxes = jnp.zeros((boxes_width,), jnp.float32)
    total_moments = MICRO + section_count - 1
    empty_act = jnp.zeros(act_shape, jnp.bfloat16)
    received = (empty_act, empty_act)
    for moment in range(total_moments):
        micro_index = moment - section_index
        active = jnp.logical_and(micro_index >= 0, micro_index < MICRO)
        slot_index = jnp.clip(micro_index, 0, MICRO - 1)
        if moment < MICRO:
            entering = whole[moment * per_micro : (moment + 1) * per_micro]
        else:
            entering = empty_act
        input_class = jnp.where(is_first, entering, received[0])
        input_boxes = jnp.where(is_first, entering, received[1])
        kept_class = store(kept_class, input_class, slot_index, active)
        kept_boxes = store(kept_boxes, input_boxes, slot_index, active)
        pre_class = (
            jnp.dot(unfold(input_class), weight_class, preferred_element_type=jnp.float32)
            + layer_bias_class
        )
        pre_boxes = (
            jnp.dot(unfold(input_boxes), weight_boxes, preferred_element_type=jnp.float32)
            + layer_bias_boxes
        )
        kept_pre_class = store(kept_pre_class, pre_class, slot_index, active)
        kept_pre_boxes = store(kept_pre_boxes, pre_boxes, slot_index, active)
        act_class = jax.nn.gelu(pre_class).astype(jnp.bfloat16).reshape(act_shape)
        act_boxes = jax.nn.gelu(pre_boxes).astype(jnp.bfloat16).reshape(act_shape)
        results = lax.cond(
            jnp.logical_and(is_final, active),
            head_pass,
            head_spare,
            act_class,
            act_boxes,
            slot_index,
        )
        grad_head_class = grad_head_class + results[0]
        grad_head_boxes = grad_head_boxes + results[1]
        grad_hbias_class = grad_hbias_class + results[2]
        grad_hbias_boxes = grad_hbias_boxes + results[3]
        head_back_class = store(head_back_class, results[4], slot_index, active)
        head_back_boxes = store(head_back_boxes, results[5], slot_index, active)
        if moment < total_moments - 1:
            received = shifted((act_class, act_boxes), "section", 1)
    grad_layer_class = jnp.zeros((patch_width, channels), jnp.float32)
    grad_layer_boxes = jnp.zeros((patch_width, channels), jnp.float32)
    grad_lbias_class = jnp.zeros((channels,), jnp.float32)
    grad_lbias_boxes = jnp.zeros((channels,), jnp.float32)
    input_back = jnp.zeros((MICRO,) + act_shape, jnp.float32)
    returned = (empty_act, empty_act)
    for moment in range(total_moments):
        micro_index = moment - (final_section - section_index)
        active = jnp.logical_and(micro_index >= 0, micro_index < MICRO)
        slot_index = jnp.clip(micro_index, 0, MICRO - 1)
        upstream_class = jnp.where(
            is_final, pick(head_back_class, slot_index), returned[0].astype(jnp.float32)
        ).reshape(pixels, channels)
        upstream_boxes = jnp.where(
            is_final, pick(head_back_boxes, slot_index), returned[1].astype(jnp.float32)
        ).reshape(pixels, channels)
        cols_class = unfold(pick(kept_class, slot_index))
        cols_boxes = unfold(pick(kept_boxes, slot_index))
        pre_class = pick(kept_pre_class, slot_index)
        pre_boxes = pick(kept_pre_boxes, slot_index)
        gelu_class = jax.vjp(jax.nn.gelu, pre_class)[1](upstream_class)[0]
        gelu_boxes = jax.vjp(jax.nn.gelu, pre_boxes)[1](upstream_boxes)[0]
        grad_pre_class = jnp.where(active, gelu_class, 0.0).astype(jnp.bfloat16)
        grad_pre_boxes = jnp.where(active, gelu_boxes, 0.0).astype(jnp.bfloat16)
        grad_layer_class = grad_layer_class + weight_grad(cols_class, grad_pre_class)
        grad_layer_boxes = grad_layer_boxes + weight_grad(cols_boxes, grad_pre_boxes)
        grad_lbias_class = grad_lbias_class + jnp.sum(grad_pre_class.astype(jnp.float32), 0)
        grad_lbias_boxes = grad_lbias_boxes + jnp.sum(grad_pre_boxes.astype(jnp.float32), 0)
        back_class = fold_back(
            input_cols(grad_pre_class, weight_class), per_micro, tile_side, channels
        )
        back_boxes = fold_back(
            input_cols(grad_pre_boxes, weight_boxes), per_micro, tile_side, channels
        )
        input_back = store(
            input_back, back_class + back_boxes, slot_index, jnp.logical_and(active, is_first)
        )
        if moment < total_moments - 1:
            returned = shifted(
                (back_class.astype(jnp.bfloat16), back_boxes.astype(jnp.bfloat16)), "section", -1
            )
    spread_back = jnp.where(
        is_first, input_back.reshape(tile_dev, tile_side, tile_side, channels), 0.0
    )
    grad_features = lax.psum_scatter(
        spread_back.astype(jnp.bfloat16), "section", scatter_dimension=1, tiled=True
    )
    summed = (
        lax.psum_scatter(grad_layer_class, "dp", scatter_dimension=0, tiled=True),
        lax.psum_scatter(grad_layer_boxes, "dp", scatter_dimension=0, tiled=True),
        lax.psum_scatter(grad_head_class, "dp", scatter_dimension=0, tiled=True),
        lax.psum_scatter(grad_head_boxes, "dp", scatter_dimension=0, tiled=True),
    )
    final_head_class, final_head_boxes = (
        lax.psum_scatter(
            summed[2].astype(jnp.bfloat16), "section", scatter_dimension=1, tiled=True
        ).astype(jnp.float32),
        lax.psum_scatter(
            summed[3].astype(jnp.bfloat16), "section", scatter_dimension=1, tiled=True
        ).astype(jnp.float32),
    )
    rows_class = lax.dynamic_update_index_in_dim(
        jnp.zeros((LAYERS, channels), jnp.float32), grad_lbias_class, section_index, 0
    )
    rows_boxes = lax.dynamic_update_index_in_dim(
        jnp.zeros((LAYERS, channels), jnp.float32), grad_lbias_boxes, section_index, 0
    )
    bias_sums = lax.psum(
        (rows_class, rows_boxes, grad_hbias_class, grad_hbias_boxes), ("section", "dp")
    )
    return (
        grad_features,
        summed[0][None],
        bias_sums[0],
        summed[1][None],
        bias_sums[1],
        final_head_class,
        bias_sums[2],
        final_head_boxes,
        bias_sums[3],
    )


def solution(mesh):
    placed = (
        P("dp", "section", None, None),
        P("section", "dp", None),
        P(),
        P("section", "dp", None),
        P(),
        P("dp", "section"),
        P(),
        P("dp", "section"),
        P(),
        P("dp", None, None),
        P("dp", None, None),
        P("dp", None, None),
        P("dp"),
    )
    return jax.shard_map(
        per_device,
        mesh=mesh,
        in_specs=placed,
        out_specs=(
            P("dp", "section", None, None),
            P("section", "dp", None),
            P(),
            P("section", "dp", None),
            P(),
            P("dp", "section"),
            P(),
            P("dp", "section"),
            P(),
        ),
        check_vma=False,
    )
```

profile of v0, /device:TPU:0, one launch (start us, length us, event | category | flops | bytes accessed | tf_op | source)
XLA Modules:
  0.0 1295.2 jit_solution(16363446263945231950)
XLA Ops:
  10.7 23.7 %all-gather = bf16[8,288,180]{1,2,0:T(8,128)(2,1)S(1)} all-gather(bf16[1,288,180]{1,2,0:T(8,128)(2,1)S(1)} %convert_bitcast_fusion), channel_id=1, replica_groups=mesh['section'=4,'dp'=8] {'dp'}, dimensions={0}, use_global_device_ids=true | all-gather | bytes 933120 | tf_op jit(solution)/shard_map/all_gather | solution.py:131
  36.7 10.4 all_gather.21
  55.8 14.3 %psum.35 = f32[]{:T(128)} all-reduce(f32[]{:T(128)} %get-tuple-element.3492), channel_id=1, replica_groups=mesh['section'=4,'dp'=8] {'dp'}, use_global_device_ids=true, to_apply=%region_1.0 | all-reduce | flops 1 | bytes 8 | tf_op jit(solution)/shard_map/psum | solution.py:126
  70.1 13.9 %all-gather.2 = bf16[8,288,9]{1,2,0:T(8,128)(2,1)S(1)} all-gather(bf16[1,288,9]{1,2,0:T(8,128)(2,1)S(1)} %convert_bitcast_fusion.1), channel_id=1, replica_groups=mesh['section'=4,'dp'=8] {'dp'}, dimensions={0}, use_global_device_ids=true | all-gather | bytes 46656 | tf_op jit(solution)/shard_map/all_gather | solution.py:132
  84.2 9.2 all-gather.3
  104.8 3.4 collective-permute-start
  110.9 4.4 collective-permute-start.3
  118.9 4.4 collective-permute-start.5
  125.1 5.0 collective-permute-start.2
  133.6 4.4 collective-permute-start.7
  142.8 4.4 collective-permute-start.9
  148.1 3.1 collective-permute-start.6
  156.2 3.5 collective-permute-start.8
  164.1 4.4 collective-permute-start.10
  189.4 5.6 conditional.13
  189.4 3.1 broadcast.6788
  195.7 7.3 conditional.12
  203.6 7.1 conditional.11
  203.6 3.2 broadcast.6740
  211.2 7.1 conditional.10
  211.2 3.1 broadcast.6716
  219.0 7.3 conditional.9
  219.0 3.2 broadcast.6692
  226.9 7.1 conditional.8
  226.9 3.2 broadcast.6668
  234.5 7.1 conditional.7
  234.5 3.2 broadcast.6642
  244.9 4.3 reduce-scatter.18.cloned.1.call-start
  249.2 18.6 %add_add_fusion = f32[2304,720]{0,1:T(8,128)} fusion(f32[2304,720]{0,1:T(8,128)} %get-tuple-element.3363, f32[2304,720]{0,1:T(8,128)} %get-tuple-element.3362, f32[2304,720]{0,1:T(8,128)} %get-tuple-element.3361, f32[2304,720]{0,1:T(8,128)} %get-tuple-element.3360, f32[2304,720]{0,1:T(8,128)} %get-tuple-element.3359, f32[2304,720]{0,1:T(8,128)} %get-tuple-element.3357, ...), kind=kLoop, calls=%fused_computation.735 | loop fusion | flops 9953280 | bytes 53084160 | tf_op jit(solution)/shard_map/add | solution.py:248
  267.8 7.9 copy.158
  311.4 3.6 add_select_fusion.27
  333.3 3.2 fusion.859
  364.7 3.6 add_select_fusion.25
  386.5 4.0 convolution_add_fusion.19
  419.9 3.6 add_select_fusion.23
  441.7 4.0 convolution_add_fusion.18
  448.2 416.0 %collective-permute-done.17 = bf16[1,16,16,256]{3,2,1,0:T(8,128)(2,1)} collective-permute-done((bf16[1,16,16,256]{3,2,1,0:T(8,128)(2,1)}, bf16[1,16,16,256]{3,2,1,0:T(8,128)(2,1)}, u32[]{:S(2)}, u32[]{:S(2)}) %collective-permute-start.17) | collective-permute-done | bytes 131104 | tf_op jit(solution)/shard_map/ppermute | solution.py:19
  884.3 24.7 %collective-permute-done.16 = bf16[1,16,16,256]{3,2,1,0:T(8,128)(2,1)} collective-permute-done((bf16[1,16,16,256]{3,2,1,0:T(8,128)(2,1)}, bf16[1,16,16,256]{3,2,1,0:T(8,128)(2,1)}, u32[]{:S(2)}, u32[]{:S(2)}) %collective-permute-start.16) | collective-permute-done | bytes 131104 | tf_op jit(solution)/shard_map/ppermute | solution.py:19
  915.9 3.7 add_select_fusion.21
  938.0 4.0 convolution_add_fusion.17
  972.5 3.7 add_select_fusion.19
  994.4 4.0 convolution_add_fusion.16
  1030.6 3.6 add_select_fusion.17
  1056.1 24.4 %collective-permute-done.22 = bf16[1,16,16,256]{3,2,1,0:T(8,128)(2,1)S(1)} collective-permute-done((bf16[1,16,16,256]{3,2,1,0:T(8,128)(2,1)S(1)}, bf16[1,16,16,256]{3,2,1,0:T(8,128)(2,1)S(1)}, u32[]{:S(2)}, u32[]{:S(2)}) %collective-permute-start.22) | collective-permute-done | bytes 131104 | tf_op jit(solution)/shard_map/ppermute | solution.py:19
  1144.1 59.4 %all-reduce.71 = bf16[288,36]{0,1:T(8,128)(2,1)S(1)} all-reduce(bf16[288,36]{0,1:T(8,128)(2,1)S(1)} %copy.161), channel_id=8, replica_groups=mesh['section'=4,'dp'=8] {'section'}, use_global_device_ids=true, to_apply=%region_61.63.clone | all-reduce | flops 10368 | bytes 41472
  1204.3 41.0 %all-reduce.73 = (f32[4,256]{1,0:T(4,128)}, f32[4,256]{1,0:T(4,128)}, f32[720]{0:T(1024)}, f32[36]{0:T(128)}) all-reduce(f32[4,256]{1,0:T(4,128)S(1)} %dynamic_update_slice.198, f32[4,256]{1,0:T(4,128)S(1)} %dynamic_update_slice.205, f32[720]{0:T(1024)S(1)} %add_add_fusion.2, ...), channel_id=1, replica_groups=mesh['section'=4,'dp'=8] {'section','dp'}, use_global_device_ids=true, to_apply=%region_47.49 | all-reduce | flops 2804 | bytes 22432 | tf_op jit(solution)/shard_map/psum | solution.py:323
  1246.8 25.0 %fusion = bf16[288,192]{0,1:T(8,128)(2,1)S(1)} fusion(bf16[288,720]{0,1:T(8,128)(2,1)S(1)} %copy.159), kind=kCustom, calls=%all-reduce-scatter | all-reduce-scatter fusion | flops 221185 | bytes 525824
  1277.3 10.6 reduce-scatter.14.cloned.1.call-done
  (1024 shorter events, 461.9 us)
Async XLA Ops:
  7.2 46.4 %copy-start = (f32[4,256]{1,0:T(4,128)S(1)}, f32[4,256]{1,0:T(4,128)}, u32[]{:S(2)}) copy-start(f32[4,256]{1,0:T(4,128)} %param.536) | copy-start | bytes 12292
  7.2 90.2 %all-gather.10.cloned.1.call-start = ((), (), s32[]{:S(2)}) async-start(), calls=%async_computation.5 | async-start | bytes 1327104 | tf_op jit(solution)/shard_map/all_gather | solution.py:130
  8.9 93.7 %all-gather.8.cloned.1.call-start = ((), (), s32[]{:S(2)}) async-start(), calls=%async_computation.4 | async-start | bytes 1327104 | tf_op jit(solution)/shard_map/all_gather | solution.py:129
  10.7 176.4 %all-gather.12.cloned.1.call-start = ((), (), s32[]{:S(2)}) async-start(), calls=%async_computation.8 | async-start | bytes 4239360 | tf_op jit(solution)/shard_map/all_gather | solution.py:137
  36.5 1106.5 %reduce-scatter.20.cloned.1.call-start = ((), (), s32[]{:S(2)}) async-start(), calls=%async_computation.10 | async-start | bytes 1327104
  52.1 18.0 %copy-start.128 = (f32[288,9]{0,1:T(8,128)S(1)}, f32[288,9]{0,1:T(8,128)}, u32[]{:S(2)}) copy-start(f32[288,9]{0,1:T(8,128)} %param.539) | copy-start | bytes 31108
  84.0 12.6 copy-start.140
  99.6 5.2 copy-start.10
  99.6 9.4 collective-permute-start.1
  104.8 10.5 collective-permute-start
  110.8 4.5 copy-start.14
  110.9 7.1 collective-permute-start.3
  118.9 4.7 copy-start.18
  118.9 11.4 collective-permute-start.5
  125.1 5.1 copy-start.16
  125.1 7.5 collective-permute-start.2
  133.6 4.7 copy-start.22
  133.6 8.3 collective-permute-start.7
  138.8 8.4 collective-permute-start.4
  142.7 4.8 copy-start.26
  142.8 8.7 collective-permute-start.9
  148.1 7.1 collective-permute-start.6
  152.4 7.6 collective-permute-start.11
  156.2 7.0 collective-permute-start.8
  164.1 5.6 copy-start.32
  164.1 6.9 collective-permute-start.10
  244.9 1000.4 %reduce-scatter.18.cloned.1.call-start = ((), (), s32[]{:S(2)}) async-start(), calls=%async_computation.9 | async-start | bytes 7962624
  305.2 32.3 %collective-permute-start.13 = (bf16[1,16,16,256]{3,2,1,0:T(8,128)(2,1)}, bf16[1,16,16,256]{3,2,1,0:T(8,128)(2,1)}, u32[]{:S(2)}, u32[]{:S(2)}) collective-permute-start(bf16[1,16,16,256]{3,2,1,0:T(8,128)(2,1)} %slice.12298), channel_id=1, source_target_pairs={{8,0},{16,8},{24,16},{9,1},{17,9},{25,17},{10,2},{18,10},{26,18},{... | collective-permute-start | bytes 393224 | tf_op jit(solution)/shard_map/ppermute | solution.py:19
  332.0 25.8 %collective-permute-start.12 = (bf16[1,16,16,256]{3,2,1,0:T(8,128)(2,1)}, bf16[1,16,16,256]{3,2,1,0:T(8,128)(2,1)}, u32[]{:S(2)}, u32[]{:S(2)}) collective-permute-start(bf16[1,16,16,256]{3,2,1,0:T(8,128)(2,1)} %slice.12299), channel_id=1, source_target_pairs={{8,0},{16,8},{24,16},{9,1},{17,9},{25,17},{10,2},{18,10},{26,18},{... | collective-permute-start | bytes 393224 | tf_op jit(solution)/shard_map/ppermute | solution.py:19
  333.3 941.0 %all-reduce.76.cloned.1.call-start = ((), (), s32[]{:S(2)}) async-start(), calls=%async_computation.11 | async-start | bytes 1048576
  356.3 36.6 %collective-permute-start.15 = (bf16[1,16,16,256]{3,2,1,0:T(8,128)(2,1)}, bf16[1,16,16,256]{3,2,1,0:T(8,128)(2,1)}, u32[]{:S(2)}, u32[]{:S(2)}) collective-permute-start(bf16[1,16,16,256]{3,2,1,0:T(8,128)(2,1)} %slice.12296), channel_id=1, source_target_pairs={{8,0},{16,8},{24,16},{9,1},{17,9},{25,17},{10,2},{18,10},{26,18},{... | collective-permute-start | bytes 393224 | tf_op jit(solution)/shard_map/ppermute | solution.py:19
  385.2 27.8 %collective-permute-start.14 = (bf16[1,16,16,256]{3,2,1,0:T(8,128)(2,1)}, bf16[1,16,16,256]{3,2,1,0:T(8,128)(2,1)}, u32[]{:S(2)}, u32[]{:S(2)}) collective-permute-start(bf16[1,16,16,256]{3,2,1,0:T(8,128)(2,1)} %slice.12297), channel_id=1, source_target_pairs={{8,0},{16,8},{24,16},{9,1},{17,9},{25,17},{10,2},{18,10},{26,18},{... | collective-permute-start | bytes 393224 | tf_op jit(solution)/shard_map/ppermute | solution.py:19
  411.7 452.5 %collective-permute-start.17 = (bf16[1,16,16,256]{3,2,1,0:T(8,128)(2,1)}, bf16[1,16,16,256]{3,2,1,0:T(8,128)(2,1)}, u32[]{:S(2)}, u32[]{:S(2)}) collective-permute-start(bf16[1,16,16,256]{3,2,1,0:T(8,128)(2,1)} %slice.12294), channel_id=1, source_target_pairs={{8,0},{16,8},{24,16},{9,1},{17,9},{25,17},{10,2},{18,10},{26,18},{... | collective-permute-start | bytes 393224 | tf_op jit(solution)/shard_map/ppermute | solution.py:19
  440.4 468.6 %collective-permute-start.16 = (bf16[1,16,16,256]{3,2,1,0:T(8,128)(2,1)}, bf16[1,16,16,256]{3,2,1,0:T(8,128)(2,1)}, u32[]{:S(2)}, u32[]{:S(2)}) collective-permute-start(bf16[1,16,16,256]{3,2,1,0:T(8,128)(2,1)} %slice.12295), channel_id=1, source_target_pairs={{8,0},{16,8},{24,16},{9,1},{17,9},{25,17},{10,2},{18,10},{26,18},{... | collective-permute-start | bytes 393224 | tf_op jit(solution)/shard_map/ppermute | solution.py:19
  880.6 28.4 %copy-start.77 = (f32[1,256,256]{2,1,0:T(8,128)S(1)}, f32[1,256,256]{2,1,0:T(8,128)}, u32[]{:S(2)}) copy-start(f32[1,256,256]{2,1,0:T(8,128)} %get-tuple-element.3569) | copy-start | bytes 786436
  883.0 61.4 %collective-permute-start.19 = (bf16[1,16,16,256]{3,2,1,0:T(8,128)(2,1)}, bf16[1,16,16,256]{3,2,1,0:T(8,128)(2,1)}, u32[]{:S(2)}, u32[]{:S(2)}) collective-permute-start(bf16[1,16,16,256]{3,2,1,0:T(8,128)(2,1)} %slice.12292), channel_id=1, source_target_pairs={{8,0},{16,8},{24,16},{9,1},{17,9},{25,17},{10,2},{18,10},{26,18},{... | collective-permute-start | bytes 393224 | tf_op jit(solution)/shard_map/ppermute | solution.py:19
  936.5 29.1 %collective-permute-start.18 = (bf16[1,16,16,256]{3,2,1,0:T(8,128)(2,1)}, bf16[1,16,16,256]{3,2,1,0:T(8,128)(2,1)}, u32[]{:S(2)}, u32[]{:S(2)}) collective-permute-start(bf16[1,16,16,256]{3,2,1,0:T(8,128)(2,1)} %slice.12293), channel_id=1, source_target_pairs={{8,0},{16,8},{24,16},{9,1},{17,9},{25,17},{10,2},{18,10},{26,18},{... | collective-permute-start | bytes 393224 | tf_op jit(solution)/shard_map/ppermute | solution.py:19
  960.8 4.8 copy-start.75
  963.2 37.7 %collective-permute-start.21 = (bf16[1,16,16,256]{3,2,1,0:T(8,128)(2,1)}, bf16[1,16,16,256]{3,2,1,0:T(8,128)(2,1)}, u32[]{:S(2)}, u32[]{:S(2)}) collective-permute-start(bf16[1,16,16,256]{3,2,1,0:T(8,128)(2,1)} %slice.12290), channel_id=1, source_target_pairs={{8,0},{16,8},{24,16},{9,1},{17,9},{25,17},{10,2},{18,10},{26,18},{... | collective-permute-start | bytes 393224 | tf_op jit(solution)/shard_map/ppermute | solution.py:19
  993.1 29.3 %collective-permute-start.20 = (bf16[1,16,16,256]{3,2,1,0:T(8,128)(2,1)}, bf16[1,16,16,256]{3,2,1,0:T(8,128)(2,1)}, u32[]{:S(2)}, u32[]{:S(2)}) collective-permute-start(bf16[1,16,16,256]{3,2,1,0:T(8,128)(2,1)} %slice.12291), channel_id=1, source_target_pairs={{8,0},{16,8},{24,16},{9,1},{17,9},{25,17},{10,2},{18,10},{26,18},{... | collective-permute-start | bytes 393224 | tf_op jit(solution)/shard_map/ppermute | solution.py:19
  1018.4 4.0 copy-start.73
  1020.9 77.6 %collective-permute-start.23 = (bf16[1,16,16,256]{3,2,1,0:T(8,128)(2,1)}, bf16[1,16,16,256]{3,2,1,0:T(8,128)(2,1)}, u32[]{:S(2)}, u32[]{:S(2)}) collective-permute-start(bf16[1,16,16,256]{3,2,1,0:T(8,128)(2,1)} %slice.12288), channel_id=1, source_target_pairs={{8,0},{16,8},{24,16},{9,1},{17,9},{25,17},{10,2},{18,10},{26,18},{... | collective-permute-start | bytes 393224 | tf_op jit(solution)/shard_map/ppermute | solution.py:19
  1050.5 30.0 %collective-permute-start.22 = (bf16[1,16,16,256]{3,2,1,0:T(8,128)(2,1)S(1)}, bf16[1,16,16,256]{3,2,1,0:T(8,128)(2,1)S(1)}, u32[]{:S(2)}, u32[]{:S(2)}) collective-permute-start(bf16[1,16,16,256]{3,2,1,0:T(8,128)(2,1)S(1)} %slice.12289), channel_id=1, source_target_pairs={{8,0},{16,8},{24,16},{9,1},{17,9},{25,17},{10,2},{18,10},{26,18},{... | collective-permute-start | bytes 393224 | tf_op jit(solution)/shard_map/ppermute | solution.py:19
  1053.8 26.7 %copy-start.72 = (f32[1,256,256]{2,1,0:T(8,128)S(1)}, f32[1,256,256]{2,1,0:T(8,128)}, u32[]{:S(2)}) copy-start(f32[1,256,256]{2,1,0:T(8,128)} %get-tuple-element.3566) | copy-start | bytes 786436
  1119.9 157.4 %reduce-scatter.16.cloned.1.call-start = ((), (), s32[]{:S(2)}) async-start(), calls=%async_computation.7 | async-start | bytes 2654208 | tf_op jit(solution)/shard_map/reduce_scatter | solution.py:305
  1124.7 163.2 %reduce-scatter.14.cloned.1.call-start = ((), (), s32[]{:S(2)}) async-start(), calls=%async_computation.6 | async-start | bytes 2654208 | tf_op jit(solution)/shard_map/reduce_scatter | solution.py:304
  1245.3 42.6 %copy-start.1 = (f32[4,256]{1,0:T(4,128)S(1)}, f32[4,256]{1,0:T(4,128)}, u32[]{:S(2)}) copy-start(f32[4,256]{1,0:T(4,128)} %param.536) | copy-start | bytes 12292
  1271.8 4.1 collective-permute-start.24
  (101 other events, 203.8 us)
Sparse Core Ops, SparseCore 0:
  10.3 29.4 all-gather.9
  41.9 22.0 all-gather.7
  65.9 52.7 all-gather.11
  245.0 536.3 reduce-scatter.19
  783.5 131.6 reduce-scatter.17
  1120.0 89.3 all-reduce.75
  1212.3 36.9 reduce-scatter.15
  1252.2 35.6 reduce-scatter.13
where the time goes:
time: 1320 us; the launch traced here: 1300 us
  waiting for transfers between devices  487 us (37%)
  other arithmetic  242 us (18%)
  local copies, waits for them, and re-layouts  219 us (17%)
  blocking collectives  197 us (15%)
  starting transfers between devices  68.8 us (5%)
  matrix products  48.7 us (4%)
  between operations  22.6 us (2%)
    ppermute x24, waiting for transfers between devices, shifted(): return lax.ppermute(block, axis, route)  476 us
    add x70, other arithmetic, fold_back(): padded = padded.at[:, row_shift:row_shift + tile_side, col_shift:col_shif...  95.5 us
    scatter-add x98, local copies, waits for them, and re-layouts, fold_back(): padded = padded.at[:, row_shift:row_shift + tile_side, col_shift:col_shif...  95.5 us
    unnamed x2, blocking collectives  84.5 us
    ppermute x24, starting transfers between devices, shifted(): return lax.ppermute(block, axis, route)  61.7 us
    unnamed x462, local copies, waits for them, and re-layouts  59.8 us
    another operation x16, other arithmetic  46.2 us
    psum x1, blocking collectives, per_device(): lax.psum((rows_class, rows_boxes, grad_hbias_class, grad_hbias_boxes), ('...  41 us
  transfers between devices with their start and end apart: 33, of which 11 were waited for; matrix products, arithmetic and copies ran while one was open for 36% of the time, Pallas kernels for 0%

commit v1 on v0

--- a/solution.py
+++ b/solution.py
@@ -1,6 +1,13 @@
+import functools
+import math
+from types import SimpleNamespace
+
 import jax
 import jax.numpy as jnp
+import numpy as np
 from jax import lax
+from jax.experimental import pallas as pl
+from jax.experimental.pallas import tpu as pltpu
 from jax.sharding import PartitionSpec as P
 
 K = 80
@@ -11,6 +18,691 @@
 
 
 huber_beta = 1.0 / 9.0
+
+F32 = jnp.float32
+BF16 = jnp.bfloat16
+MESH = pl.DeviceIdType.MESH
+GELU_C = math.sqrt(2.0 / math.pi)
+
+SECTIONS = 4
+PLANES = 4
+CORES = 2
+CH = 256
+PX = TILE * TILE
+ROWS = 288
+HALF = ROWS // 2
+PACK = ROWS + HALF
+LANES = 128
+TAIL = 64
+HEAD = SECTIONS * (LANES + TAIL)
+LAB = 256
+TGT = 640
+DEEP = 9 * CH
+
+
+def head_layout(width):
+    per = width // SECTIONS
+    columns = np.full((HEAD,), -1)
+    for s in range(SECTIONS):
+        main = min(per, LANES)
+        columns[s * LANES : s * LANES + main] = s * per + np.arange(main)
+        rest = per - main
+        at = SECTIONS * LANES + s * TAIL
+        columns[at : at + rest] = s * per + main + np.arange(rest)
+    return columns
+
+
+def constants(class_width, boxes_width):
+    classes, boxes = head_layout(class_width), head_layout(boxes_width)
+    spread = np.zeros((2, LAB, HEAD), np.float32)
+    targets = np.zeros((TGT, HEAD), np.float32)
+    for j in range(TILE):
+        for col in range(HEAD):
+            if classes[col] >= 0:
+                spread[0, j * A + classes[col] // K, col] = 1
+            if boxes[col] >= 0:
+                spread[1, j * A + boxes[col] // 4, col] = 1
+                targets[j * boxes_width + boxes[col], col] = 1
+    pixel = np.arange(PX)[:, None] % TILE
+    mask_lab = (np.arange(LAB)[None, :] // A == pixel) & (np.arange(LAB)[None, :] < TILE * A)
+    mask_tgt = (np.arange(TGT)[None, :] // boxes_width == pixel) & (np.arange(TGT)[None, :] < TILE * boxes_width)
+    label = np.where(classes >= 0, classes % K, -9).astype(np.float32)[None, :] + 2.0
+    bf = lambda v: jnp.asarray(v.astype(np.float32), BF16)
+    return bf(spread), bf(targets), bf(mask_lab), bf(mask_tgt), jnp.asarray(np.repeat(label, 8, 0))
+
+
+def dot(a, b):
+    return jnp.dot(a, b, preferred_element_type=F32)
+
+
+def dot_nt(a, b):
+    return lax.dot_general(a, b, (((1,), (1,)), ((), ())), preferred_element_type=F32)
+
+
+def put_shifted(ref, t, v, order, width):
+    col = lax.broadcasted_iota(jnp.int32, v.shape, 0) % TILE
+    before = jnp.where(col == 0, 0.0, pltpu.roll(v, 1, 0))
+    after = jnp.where(col == TILE - 1, 0.0, pltpu.roll(v, PX - 1, 0))
+    blocks = (before, v, after) if order > 0 else (after, v, before)
+    for s, block in enumerate(blocks):
+        ref[t, TILE : TILE + PX, s * width : (s + 1) * width] = block.astype(BF16)
+
+
+def shifted_rows(ref, r, lanes=slice(None)):
+    return ref[:, TILE * r : TILE * r + PX, lanes].reshape(2 * PX, -1)
+
+
+def swap_halves(p, q):
+    p, q = p.astype(F32), q.astype(F32)
+    low = lax.broadcasted_iota(jnp.int32, p.shape, 1) < TAIL
+    p_turned, q_turned = pltpu.roll(p, TAIL, 1), pltpu.roll(q, TAIL, 1)
+    return jnp.where(low, p, q_turned), jnp.where(low, p_turned, q)
+
+
+def forward_layer(m, l):
+    z = sum(dot(shifted_rows(m.act3, r), m.w[l, 3 * CH * r : 3 * CH * (r + 1), :]) for r in range(3))
+    z = z + m.bias[m.role, l : l + 1, 0:CH]
+    for t in range(2):
+        zt = z[t * PX : (t + 1) * PX]
+        square = zt * zt
+        th = jnp.tanh(GELU_C * (zt + 0.044715 * zt * square))
+        half = 0.5 * (1.0 + th)
+        a = zt * half
+        m.slope[l, t * PX : (t + 1) * PX, :] = half + (0.5 * GELU_C) * zt * (1.0 - th * th) * (
+            1.0 + (3 * 0.044715) * square
+        )
+        put_shifted(m.act3, t, a, 1, CH)
+        m.act_t[l + 1, :, t * PX : (t + 1) * PX] = a.T.astype(BF16)
+
+
+def head_forward(m):
+    for n in range(0, HEAD, 256):
+        m.logits[:, n : n + 256] = sum(
+            dot(shifted_rows(m.act3, r), m.wh[3 * CH * r : 3 * CH * (r + 1), n : n + 256]) for r in range(3)
+        )
+
+
+def expand(row, mask):
+    lanes = row.shape[-1]
+    return jnp.broadcast_to(row[:, None, :], (TILE, TILE, lanes)).reshape(PX, lanes) * mask[...].astype(F32)
+
+
+def prepare_loss(m):
+    for t, lab in enumerate((m.lab, m.lab_in)):
+        codes = expand(lab[:, 0:LAB], m.mask_lab).astype(BF16)
+        m.code[t * PX : (t + 1) * PX, :] = dot(codes, m.spread[m.role])
+
+    @pl.when(m.role == 1)
+    def _():
+        for t, lab in enumerate((m.lab, m.lab_in)):
+            values = expand(lab[:, LAB : LAB + TGT], m.mask_tgt)
+            m.target[t * PX : (t + 1) * PX, :] = jnp.dot(
+                values, m.targets[...].astype(F32), precision=lax.Precision.HIGHEST, preferred_element_type=F32
+            )
+
+
+def loss_gradient(m):
+    total = m.count_sum[0:1, :] + m.count_in[1, 0:1, :] + m.count_in[2, 0:1, :] + m.count_in[3, 0:1, :]
+    scale = jnp.concatenate([1.0 / jnp.maximum(total, 1.0)] * (HEAD // LANES), axis=1)
+    bias = m.bias[m.role, 4:5, :]
+
+    def keep(t, g):
+        g = g.astype(BF16).astype(F32)
+        m.grad_bias[4:5, :] += jnp.sum(g, axis=0, keepdims=True)
+        put_shifted(m.g3h, t, g, -1, HEAD)
+
+    @pl.when(m.role == 0)
+    def _():
+        for t in range(2):
+            at = slice(t * PX, (t + 1) * PX)
+            x = m.logits[at, :] + bias
+            code = m.code[at, :]
+            labeled = code == m.label[0:1, :]
+            y = jnp.where(labeled, -x, x)
+            e = jnp.exp(-jnp.abs(y))
+            q = jnp.where(y >= 0, 1.0, e) / (1.0 + e)
+            softplus = jnp.maximum(y, 0.0) + jnp.log1p(e)
+            slope = q * q * (2.0 * (1.0 - q) * softplus + q)
+            keep(t, slope * jnp.where(labeled, -0.25, jnp.where(code > 0.5, 0.75, 0.0)) * scale)
+
+    @pl.when(m.role == 1)
+    def _():
+        for t in range(2):
+            at = slice(t * PX, (t + 1) * PX)
+            offset = m.logits[at, :] + bias - m.target[at, :]
+            keep(t, jnp.where(m.code[at, :] > 1.5, jnp.clip(offset / huber_beta, -1.0, 1.0), 0.0) * scale)
+
+
+def head_kernel_gradient(m, r):
+    for s in range(3):
+        at = (3 * r + s) * CH
+        m.gh[at : at + CH, :] = dot(
+            m.act_t[LAYERS], shifted_rows(m.g3h, 2 - r, slice(s * HEAD, (s + 1) * HEAD))
+        ).astype(BF16)
+
+
+def input_gradient(m, g3, width, kernel):
+    acc = None
+    for r in range(3):
+        for s in range(3):
+            at = (3 * r + s) * CH
+            part = dot_nt(shifted_rows(g3, 2 - r, slice(s * width, (s + 1) * width)), kernel[at : at + CH, :])
+            acc = part if acc is None else acc + part
+    return acc
+
+
+def layer_upstream(m, l):
+    g = (m.da[...] * m.slope[l]).astype(BF16).astype(F32)
+    m.grad_bias[l : l + 1, 0:CH] = jnp.sum(g, axis=0, keepdims=True)
+    for t in range(2):
+        put_shifted(m.g3, t, g[t * PX : (t + 1) * PX], -1, CH)
+
+
+def layer_kernel_gradient(m, l, r):
+    part = dot(m.act_t[l], shifted_rows(m.g3, 2 - r))
+    for s in range(3):
+        at = (3 * r + s) * CH
+        m.g[l, at : at + CH, :] = part[:, s * CH : (s + 1) * CH].astype(BF16)
+
+
+class Traffic:
+    def __init__(self, send_sem, recv_sem):
+        self.send_sem, self.recv_sem = send_sem, recv_sem
+        self.names, self.used, self.sent = {}, 0, []
+
+    def copy(self, name, src, dst, peer, span=1, offset=0):
+        if name not in self.names:
+            self.names[name] = self.used
+            self.used += span
+        i = self.names[name] + offset
+        return pltpu.make_async_remote_copy(
+            src, dst, self.send_sem.at[i], self.recv_sem.at[i], device_id=peer, device_id_type=MESH
+        )
+
+    def send(self, name, src, dst, peer, when=None, **at):
+        copy = self.copy(name, src, dst, peer, **at)
+        if when is None:
+            copy.start()
+        else:
+            pl.when(when)(copy.start)
+        self.sent.append((when, copy))
+
+    def arrived(self, name, dst, peer, **at):
+        self.copy(name, dst, dst, peer, **at).wait_recv()
+
+    def finish(self):
+        for when, copy in self.sent:
+            if when is None:
+                copy.wait_send()
+            else:
+                pl.when(when)(copy.wait_send)
+
+
+SEMAPHORES = 192
+GATHER_ORDER = (
+    ("T", 0, "A"), ("H", 0, "B"), ("T", 1, "B"), ("T", 3, "A"), ("T", 2, "B"), ("H", 1, "A"), ("H", 3, "B"), ("H", 2, "A"),
+)
+
+
+def head_kernel(
+    features, tower_class, tower_boxes, head_class, head_boxes, bias, state, labels, targets_in, valid,
+    spread, targets, mask_lab, mask_tgt, label,
+    out_features, out_class, out_boxes, out_head_class, out_head_boxes, out_bias,
+    own, own_h, w, wh, hp, g, gh, rc, rch, sh, r1, r1h, r2, r2h, rz, rzh,
+    act3, g3, g3h, act_t, slope, logits, code, target, da,
+    x, lab, lab_in, count_mine, count_sum, count_in, grad_bias, bias_in, bias_z, dx, dx_in, tile_out, features_in,
+    send_sem, recv_sem,
+):
+    s, dp = lax.axis_index("section"), lax.axis_index("dp")
+    my_y, my_x, my_z, my_c = s // 2, s % 2, dp // 2, dp % 2
+    sx, sy, sg = 2 * my_y + (1 - my_x), 2 * (1 - my_y) + my_x, 2 * (1 - my_y) + (1 - my_x)
+    to_x, to_y, to_g, to_c = (sx, dp), (sy, dp), (sg, dp), (s, 2 * my_z + 1 - my_c)
+    plane = lambda k: (my_z + k) % PLANES
+    to_z = lambda k: (s, 2 * plane(k) + my_c)
+    to_pair = (s, 2 * (my_z + 1 - 2 * (my_z % 2)) + my_c)
+    role = my_z % 2
+    net = Traffic(send_sem, recv_sem)
+    m = SimpleNamespace(
+        w=w, wh=wh, g=g, gh=gh, act3=act3, g3=g3, g3h=g3h, act_t=act_t, slope=slope, logits=logits, code=code,
+        target=target, da=da, lab=lab, lab_in=lab_in, count_sum=count_sum, count_in=count_in, grad_bias=grad_bias,
+        bias=bias, spread=spread, targets=targets, mask_lab=mask_lab, mask_tgt=mask_tgt, label=label, role=role,
+    )
+
+    def shard(z, c):
+        return pl.ds(pl.multiple_of(ROWS * (2 * z + c), 16), ROWS)
+
+    barrier = pltpu.get_barrier_semaphore()
+    peers = (to_x, to_y, to_g, to_c, to_z(1), to_z(2), to_z(3))
+    for peer in peers:
+        pl.semaphore_signal(barrier, inc=1, device_id=peer, device_id_type=MESH)
+
+    for role_at, (tower, head) in enumerate(((tower_class, head_class), (tower_boxes, head_boxes))):
+        own[role_at] = tower[0].astype(BF16)
+        width = head.shape[1]
+        main = min(width, LANES)
+        own_h[role_at] = jnp.zeros((PACK, LANES), BF16)
+        own_h[role_at, 0:ROWS, 0:main] = head[:, 0:main].astype(BF16)
+        if width > LANES:
+            logits[0:ROWS, 0:LANES] = jnp.zeros((ROWS, LANES), F32)
+            logits[0:ROWS, 0 : width - LANES] = head[:, LANES:width]
+            own_h[role_at, ROWS:PACK, :] = (
+                logits[0:HALF, 0:LANES] + pltpu.roll(logits[HALF:ROWS, 0:LANES], TAIL, 1)
+            ).astype(BF16)
+
+    row = lax.broadcasted_iota(jnp.int32, (TILE, TILE * A), 0)
+    found = jnp.zeros((TILE, TILE * A), F32)
+    for t in range(SECTIONS):
+        found += jnp.where(jnp.logical_and(state[t] == 1, row < valid[t]), 1.0, 0.0)
+    count_mine[...] = jnp.full((8, LANES), jnp.sum(found), F32)
+    inside = row < valid[s]
+    kind = state[s]
+    lab[...] = jnp.zeros_like(lab)
+    lab[:, 0 : TILE * A] = jnp.where(
+        inside,
+        jnp.where(kind == 1, labels[s].astype(F32) + 2.0, jnp.where(kind == 2, 0.0, 1.0)),
+        0.0,
+    )
+    lab[:, LAB : LAB + targets_in.shape[2]] = targets_in[s]
+
+    pl.semaphore_wait(barrier, len(peers))
+
+    for kind_name, src, dst in (("T", own, w), ("H", own_h, hp)):
+        for k in (1, 3, 2):
+            at = dst.at[s, shard(my_z, my_c), :] if kind_name == "T" else dst.at[s, my_z]
+            net.send(("z", kind_name, k), src.at[plane(k) % 2], at, to_z(k))
+        if kind_name == "T":
+            for name, peer, sec in (("x", to_x, sx), ("y", to_y, sy), ("g", to_g, sg)):
+                net.send(("f", name), features.at[sec], x.at[0, pl.ds(pl.multiple_of(64 * s, 64), 64), :], peer)
+            net.send("count c", count_mine, count_in.at[0], to_c)
+            net.send("lab", lab, lab_in, to_pair)
+    w[s, shard(my_z, my_c), :] = own[role]
+    hp[s, my_z] = own_h[role]
+
+    def piece(kind_name, sec, j):
+        z = (my_z + PLANES - j) % PLANES
+        return w.at[sec, shard(z, my_c), :] if kind_name == "T" else hp.at[sec, z]
+
+    def ways(way):
+        return ((to_x, sx), (to_y, sy)) if way == "A" else ((to_y, sy), (to_x, sx))
+
+    def gather_first(kind_name, j, way):
+        (n1, s1), (n2, s2) = ways(way)
+        if j:
+            net.arrived(("z", kind_name, j), piece(kind_name, s, j), to_z(PLANES - j))
+        mine = piece(kind_name, s, j)
+        net.send(("g1", kind_name, j), mine, mine, n1)
+        if kind_name == "T":
+            net.send(("swap", kind_name, j, 0), mine, mine, to_c)
+
+    def gather_second(kind_name, j, way):
+        (n1, s1), (n2, s2) = ways(way)
+        mine, first = piece(kind_name, s, j), piece(kind_name, s1, j)
+        net.send(("g2", kind_name, j), mine, mine, n2)
+        net.arrived(("g1", kind_name, j), first, n1)
+        net.send(("g3", kind_name, j), first, first, n2)
+        if kind_name == "T":
+            net.send(("swap", kind_name, j, 1), first, first, to_c)
+
+    def gather_third(kind_name, j, way):
+        (n1, s1), (n2, s2) = ways(way)
+        for i, (name, sec) in enumerate((("g2", s2), ("g3", sg))):
+            got = piece(kind_name, sec, j)
+            net.arrived((name, kind_name, j), got, n2)
+            if kind_name == "T":
+                net.send(("swap", kind_name, j, 2 + i), got, got, to_c)
+        if kind_name == "H":
+            z = (my_z + PLANES - j) % PLANES
+            at = pl.multiple_of(ROWS * (2 * z + my_c), 16)
+            for sec in range(SECTIONS):
+                wh[pl.ds(at, ROWS), sec * LANES : (sec + 1) * LANES] = hp[sec, z, 0:ROWS, :]
+            for q in range(2):
+                lanes = slice((SECTIONS + q) * LANES, (SECTIONS + q + 1) * LANES)
+                top, bottom = swap_halves(hp[2 * q, z, ROWS:PACK, :], hp[2 * q + 1, z, ROWS:PACK, :])
+                wh[pl.ds(at, HALF), lanes] = top.astype(BF16)
+                wh[pl.ds(at + HALF, HALF), lanes] = bottom.astype(BF16)
+            block = wh.at[pl.ds(at, ROWS), :]
+            net.send(("swap", "H", j), block, block, to_c)
+
+    def swapped(kind_name, j):
+        z = (my_z + PLANES - j) % PLANES
+        if kind_name == "H":
+            net.arrived(("swap", "H", j), wh.at[shard(z, 1 - my_c), :], to_c)
+            return
+        (_, s1), (_, s2) = ways(dict((entry[:2], entry[2]) for entry in GATHER_ORDER)[(kind_name, j)])
+        for i, sec in enumerate((s, s1, s2, sg)):
+            net.arrived(("swap", "T", j, i), w.at[sec, shard(z, 1 - my_c), :], to_c)
+
+    def start():
+        for ref in (act3, g3, g3h):
+            for t in range(2):
+                ref[t, 0:TILE, :] = jnp.zeros((TILE, ref.shape[2]), BF16)
+                ref[t, TILE + PX : 2 * TILE + PX, :] = jnp.zeros((TILE, ref.shape[2]), BF16)
+        grad_bias[...] = jnp.zeros_like(grad_bias)
+        x[0, pl.ds(pl.multiple_of(64 * s, 64), 64), :] = features[s]
+        for name, peer, sec in (("x", to_x, sx), ("y", to_y, sy), ("g", to_g, sg)):
+            net.arrived(("f", name), x.at[0, pl.ds(pl.multiple_of(64 * sec, 64), 64), :], peer)
+        net.send("tile", x.at[0], x.at[1], to_pair)
+        net.arrived("count c", count_in.at[0], to_c)
+        count_sum[...] = count_mine[...] + count_in[0]
+        for k in (1, 2, 3):
+            net.send(("count", k), count_sum, count_in.at[k], to_z(k))
+
+    def prepare():
+        net.arrived("lab", lab_in, to_pair)
+        prepare_loss(m)
+        net.arrived("tile", x.at[1], to_pair)
+        for t in range(2):
+            v = x[t].astype(F32)
+            put_shifted(act3, t, v, 1, CH)
+            act_t[0, :, t * PX : (t + 1) * PX] = v.T.astype(BF16)
+
+    stages = len(GATHER_ORDER) + 2
+    towers_done = max(i for i, entry in enumerate(GATHER_ORDER) if entry[0] == "T") + 2
+    for i in range(stages):
+        if i < len(GATHER_ORDER):
+            gather_first(*GATHER_ORDER[i])
+        if 1 <= i < len(GATHER_ORDER) + 1:
+            gather_second(*GATHER_ORDER[i - 1])
+        if i >= 2:
+            gather_third(*GATHER_ORDER[i - 2])
+        if i == 1:
+            start()
+        if i == 2:
+            prepare()
+        if i == towers_done:
+            for j in range(PLANES):
+                swapped("T", j)
+        if towers_done <= i < towers_done + LAYERS:
+            forward_layer(m, i - towers_done)
+    for l in range(max(0, stages - towers_done), LAYERS):
+        forward_layer(m, l)
+    for k in (1, 2, 3):
+        net.arrived(("count", k), count_in.at[k], to_z(PLANES - k))
+    for j in range(PLANES):
+        swapped("H", j)
+
+    def summed(refs_into, refs_from):
+        refs_into[...] = (refs_into[...].astype(F32) + refs_from[...].astype(F32)).astype(BF16)
+
+    def reduce_start(l, zp):
+        if l is None:
+            net.send(("rc", l, zp), gh.at[shard(zp, 1 - my_c), :], rch.at[zp], to_c)
+        else:
+            net.send(("rc", l, zp), g.at[l, shard(zp, 1 - my_c), :], rc.at[l, zp], to_c)
+
+    def bound(l, zp):
+        x_here, y_here = my_x == l % 2, my_y == l // 2
+        if zp < 2:
+            return x_here, y_here, to_x, to_y
+        return y_here, x_here, to_y, to_x
+
+    def buffers(kind_name, l, zp):
+        if kind_name == "T":
+            return rc.at[l, zp], r1.at[l, zp], r2.at[zp]
+        return sh.at[l, zp], r1h.at[l, zp], r2h.at[zp]
+
+    def reduce_first_send(kind_name, l, zp):
+        here1, here2, n1, n2 = bound(l, zp)
+        mine, into1, into2 = buffers(kind_name, l, zp)
+        away = jnp.logical_not(here1)
+
+        net.send(("r1", kind_name, l, zp), mine, into1, n1, away)
+
+    def reduce_cores_tower(l, zp):
+        net.arrived(("rc", l, zp), rc.at[l, zp], to_c)
+        rc[l, zp] = (rc[l, zp].astype(F32) + g[l, shard(zp, my_c), :].astype(F32)).astype(BF16)
+        reduce_first_send("T", l, zp)
+
+    def reduce_cores_head(zp):
+        net.arrived(("rc", None, zp), rch.at[zp], to_c)
+        at = pl.multiple_of(ROWS * (2 * zp + my_c), 16)
+        for sec in range(SECTIONS):
+            lanes = slice(sec * LANES, (sec + 1) * LANES)
+            sh[sec, zp, 0:ROWS, :] = (
+                rch[zp, :, lanes].astype(F32) + gh[pl.ds(at, ROWS), lanes].astype(F32)
+            ).astype(BF16)
+        for q in range(2):
+            lanes = slice((SECTIONS + q) * LANES, (SECTIONS + q + 1) * LANES)
+            top = rch[zp, 0:HALF, lanes].astype(F32) + gh[pl.ds(at, HALF), lanes].astype(F32)
+            bottom = rch[zp, HALF:ROWS, lanes].astype(F32) + gh[pl.ds(at + HALF, HALF), lanes].astype(F32)
+            first, second = swap_halves(top, bottom)
+            sh[2 * q, zp, ROWS:PACK, :] = first.astype(BF16)
+            sh[2 * q + 1, zp, ROWS:PACK, :] = second.astype(BF16)
+        for sec in range(SECTIONS):
+            reduce_first_send("H", sec, zp)
+
+    def reduce_second(kind_name, l, zp):
+        here1, here2, n1, n2 = bound(l, zp)
+        mine, into1, into2 = buffers(kind_name, l, zp)
+
+        @pl.when(here1)
+        def _():
+            net.arrived(("r1", kind_name, l, zp), into1, n1)
+            summed(mine, into1)
+
+        away = jnp.logical_and(here1, jnp.logical_not(here2))
+
+        net.send(("r2", kind_name, zp), mine, into2, n2, away)
+
+    def reduce_third(kind_name, l, zp):
+        here1, here2, n1, n2 = bound(l, zp)
+        mine, into1, into2 = buffers(kind_name, l, zp)
+
+        @pl.when(s == l)
+        def _():
+            net.arrived(("r2", kind_name, zp), into2, n2)
+            summed(mine, into2)
+
+        away = jnp.logical_and(s == l, my_z != zp)
+        out = rz if kind_name == "T" else rzh
+        k = (zp + PLANES - my_z) % PLANES
+        net.send(("rz", kind_name), mine, out.at[my_z], (s, 2 * zp + my_c), away, span=PLANES, offset=k)
+
+    def collect(kind_name):
+        mine, others = (rc, rz) if kind_name == "T" else (sh, rzh)
+        for k in (1, 2, 3):
+            source = plane(PLANES - k)
+            net.arrived(("rz", kind_name), others.at[source], to_z(PLANES - k), span=PLANES, offset=k)
+        same = mine[s, my_z].astype(F32) + others[plane(2)].astype(F32)
+        return same, others[plane(1)].astype(F32) + others[plane(3)].astype(F32)
+
+    def by_role(same, other, store):
+        @pl.when(role == 0)
+        def _():
+            store(same, other)
+
+        @pl.when(role == 1)
+        def _():
+            store(other, same)
+
+    def store_towers(of_class, of_boxes):
+        out_class[0] = of_class
+        out_boxes[0] = of_boxes
+
+    def store_heads(of_class, of_boxes):
+        for packed, out in ((of_class, out_head_class), (of_boxes, out_head_boxes)):
+            width = out.shape[1]
+            main, rest = min(width, LANES), max(0, width - LANES)
+            out[:, 0:main] = packed[0:ROWS, 0:main]
+            if rest:
+                out[0:HALF, LANES:width] = packed[ROWS:PACK, 0:rest]
+                out[HALF:ROWS, LANES:width] = pltpu.roll(packed[ROWS:PACK, :], TAIL, 1)[:, 0:rest]
+
+    head_forward(m)
+    loss_gradient(m)
+    for r in range(3):
+        head_kernel_gradient(m, r)
+        for zp in ((0,), (1,), (2, 3))[r]:
+            reduce_start(None, zp)
+        if r:
+            reduce_cores_head(r - 1)
+    da[...] = input_gradient(m, g3h, HEAD, wh)
+    reduce_cores_head(2)
+    reduce_cores_head(3)
+    for l in range(LAYERS - 1, -1, -1):
+        layer_upstream(m, l)
+        if l == 0:
+            net.send("bias c", grad_bias, bias_in.at[0], to_c)
+        for r in range(3):
+            layer_kernel_gradient(m, l, r)
+            for zp in ((0,), (1,), (2, 3))[r]:
+                reduce_start(l, zp)
+        da[...] = input_gradient(m, g3, CH, w.at[l])
+        if l == 0:
+            dx[...] = da[PX : 2 * PX, :].astype(BF16)
+            net.send("dx", dx, dx_in, to_pair)
+        for zp in range(PLANES):
+            reduce_cores_tower(l, zp)
+
+    net.arrived("bias c", bias_in.at[0], to_c)
+    bias_z[0] = grad_bias[...] + bias_in[0]
+    net.send("bias x", bias_z.at[0], bias_in.at[1], to_x)
+
+    for zp in range(PLANES):
+        for sec in range(SECTIONS):
+            reduce_second("H", sec, zp)
+    net.arrived("bias x", bias_in.at[1], to_x)
+    bias_z[1] = bias_z[0] + bias_in[1]
+    net.send("bias y", bias_z.at[1], bias_in.at[2], to_y)
+
+    net.arrived("dx", dx_in, to_pair)
+    tile_out[...] = (da[0:PX, :] + dx_in[...].astype(F32)).astype(BF16)
+    mine_at = pl.ds(pl.multiple_of(64 * s, 64), 64)
+    for name, peer, sec in (("x", to_x, sx), ("y", to_y, sy), ("g", to_g, sg)):
+        net.send(
+            ("b", name), tile_out.at[pl.ds(pl.multiple_of(64 * sec, 64), 64), :], features_in.at[s], peer
+        )
+    for l in range(LAYERS - 1, -1, -1):
+        for zp in range(PLANES):
+            reduce_second("T", l, zp)
+        if l == LAYERS - 1:
+            net.arrived("bias y", bias_in.at[2], to_y)
+            bias_z[2] = bias_z[1] + bias_in[2]
+            for k in (1, 2, 3):
+                net.send(("bias z", k), bias_z.at[2], bias_in.at[2 + k], to_z(k))
+            for zp in range(PLANES):
+                for sec in range(SECTIONS):
+                    reduce_third("H", sec, zp)
+        else:
+            for zp in range(PLANES):
+                reduce_third("T", l + 1, zp)
+    for name, peer, sec in (("x", to_x, sx), ("y", to_y, sy), ("g", to_g, sg)):
+        net.arrived(("b", name), features_in.at[sec], peer)
+        out_features[sec] = features_in[sec]
+    out_features[s] = tile_out[mine_at, :]
+    for k in (1, 2, 3):
+        net.arrived(("bias z", k), bias_in.at[2 + k], to_z(PLANES - k))
+    out_bias[role] = bias_z[2] + bias_in[4]
+    out_bias[1 - role] = bias_in[3] + bias_in[5]
+    by_role(*collect("H"), store_heads)
+    for zp in range(PLANES):
+        reduce_third("T", 0, zp)
+    by_role(*collect("T"), store_towers)
+    net.finish()
+
+
+def fast(features, tower_class, bias_class, tower_boxes, bias_boxes, head_class, head_class_bias, head_boxes,
+         head_boxes_bias, anchor_state, class_labels, box_targets, valid_rows):
+    class_width, boxes_width = head_class_bias.shape[0], head_boxes_bias.shape[0]
+
+    def lay(vector):
+        parts = vector.reshape(SECTIONS, -1)
+        main = parts[:, :LANES]
+        rest = parts[:, LANES:]
+        main = jnp.pad(main, ((0, 0), (0, LANES - main.shape[1]))).reshape(-1)
+        rest = jnp.pad(rest, ((0, 0), (0, TAIL - rest.shape[1]))).reshape(-1)
+        return jnp.concatenate([main, rest])[None]
+
+    def unlay(row, width):
+        per = width // SECTIONS
+        main = row[: SECTIONS * LANES].reshape(SECTIONS, LANES)[:, : min(per, LANES)]
+        rest = row[SECTIONS * LANES :].reshape(SECTIONS, TAIL)[:, : max(0, per - LANES)]
+        return jnp.concatenate([main, rest], axis=1).reshape(width)
+
+    bias = jnp.stack(
+        [
+            jnp.concatenate([jnp.pad(tower, ((0, 0), (0, HEAD - CH))), lay(head), jnp.zeros((3, HEAD), F32)])
+            for tower, head in ((bias_class, head_class_bias), (bias_boxes, head_boxes_bias))
+        ]
+    )
+    tiles = features.shape[0]
+    vmem = pl.BlockSpec(memory_space=pltpu.VMEM)
+    smem = pl.BlockSpec(memory_space=pltpu.SMEM)
+    v = lambda shape, dtype: pltpu.VMEM(shape, dtype)
+    out = lambda shape, dtype: jax.ShapeDtypeStruct(shape, dtype)
+    results = pl.pallas_call(
+        head_kernel,
+        out_shape=(
+            out((tiles, 64, CH), BF16),
+            out((1, ROWS, CH), F32),
+            out((1, ROWS, CH), F32),
+            out(head_class.shape, F32),
+            out(head_boxes.shape, F32),
+            out((2, 8, HEAD), F32),
+        ),
+        in_specs=[vmem] * 9 + [smem] + [vmem] * 5,
+        out_specs=(vmem,) * 6,
+        scratch_shapes=[
+            v((2, ROWS, CH), BF16),
+            v((2, PACK, LANES), BF16),
+            v((LAYERS, DEEP, CH), BF16),
+            v((DEEP, HEAD), BF16),
+            v((SECTIONS, PLANES, PACK, LANES), BF16),
+            v((LAYERS, DEEP, CH), BF16),
+            v((DEEP, HEAD), BF16),
+            v((LAYERS, PLANES, ROWS, CH), BF16),
+            v((PLANES, ROWS, HEAD), BF16),
+            v((SECTIONS, PLANES, PACK, LANES), BF16),
+            v((LAYERS, PLANES, ROWS, CH), BF16),
+            v((SECTIONS, PLANES, PACK, LANES), BF16),
+            v((PLANES, ROWS, CH), BF16),
+            v((PLANES, PACK, LANES), BF16),
+            v((PLANES, ROWS, CH), BF16),
+            v((PLANES, PACK, LANES), BF16),
+            v((2, PX + 2 * TILE, 3 * CH), BF16),
+            v((2, PX + 2 * TILE, 3 * CH), BF16),
+            v((2, PX + 2 * TILE, 3 * HEAD), BF16),
+            v((LAYERS + 1, CH, 2 * PX), BF16),
+            v((LAYERS, 2 * PX, CH), F32),
+            v((2 * PX, HEAD), F32),
+            v((2 * PX, HEAD), F32),
+            v((2 * PX, HEAD), F32),
+            v((2 * PX, CH), F32),
+            v((2, PX, CH), BF16),
+            v((TILE, LAB + TGT), F32),
+            v((TILE, LAB + TGT), F32),
+            v((8, LANES), F32),
+            v((8, LANES), F32),
+            v((4, 8, LANES), F32),
+            v((8, HEAD), F32),
+            v((6, 8, HEAD), F32),
+            v((3, 8, HEAD), F32),
+            v((PX, CH), BF16),
+            v((PX, CH), BF16),
+            v((PX, CH), BF16),
+            v((SECTIONS, 64, CH), BF16),
+            pltpu.SemaphoreType.DMA((SEMAPHORES,)),
+            pltpu.SemaphoreType.DMA((SEMAPHORES,)),
+        ],
+        compiler_params=pltpu.CompilerParams(
+            collective_id=0, has_side_effects=True, vmem_limit_bytes=62 * 2**20
+        ),
+    )(
+        features.reshape(tiles, 64, CH), tower_class, tower_boxes, head_class, head_boxes, bias,
+        anchor_state, class_labels, box_targets, valid_rows, *constants(class_width, boxes_width),
+    )
+    grad_features, grad_class, grad_boxes, grad_head_class, grad_head_boxes, sums = results
+    return (
+        grad_features.reshape(features.shape),
+        grad_class,
+        sums[0, :LAYERS, :CH],
+        grad_boxes,
+        sums[1, :LAYERS, :CH],
+        grad_head_class,
+        unlay(sums[0, LAYERS], class_width),
+        grad_head_boxes,
+        unlay(sums[1, LAYERS], boxes_width),
+    )
 
 
 def shifted(block, axis, distance):
@@ -337,6 +1029,7 @@
 
 
 def solution(mesh):
+    fits = mesh.shape["section"] == SECTIONS == LAYERS and mesh.shape["dp"] == PLANES * CORES
     placed = (
         P("dp", "section", None, None),
         P("section", "dp", None),
@@ -353,7 +1046,7 @@
         P("dp"),
     )
     return jax.shard_map(
-        per_device,
+        fast if fits else per_device,
         mesh=mesh,
         in_specs=placed,
         out_specs=(

time: 1320 us -> 154 us (0.12); the launches traced: 1300 us -> 153 us
  waiting for transfers between devices: 487 us -> 0 us
  other arithmetic: 242 us -> 1.41 us
  local copies, waits for them, and re-layouts: 219 us -> 14.1 us
  blocking collectives: 197 us -> 0 us
  Pallas kernels: 0 us -> 136 us
  starting transfers between devices: 68.8 us -> 0 us
  matrix products: 48.7 us -> 0 us
  between operations: 22.6 us -> 0.7 us
    ppermute x24 -> x0, waiting for transfers between devices: 476 us -> none  [shifted(): return lax.ppermute(block, axis, route)]
    pallas_call x0 -> x1, Pallas kernels: none -> 136 us  [fast(): pl.pallas_call(head_kernel, out_shape=(out((tiles, 64, CH), BF16), out((1...]
    add x76 -> x0, other arithmetic: 116 us -> none  [the longest x70 95.5 us: fold_back(): padded = padded.at[:, row_shift:row_shift + tile_side, col_shift:col_shif...]
    scatter-add x98 -> x0, local copies, waits for them, and re-layouts: 95.5 us -> none  [fold_back(): padded = padded.at[:, row_shift:row_shift + tile_side, col_shift:col_shif...]
    unnamed x2 -> x0, blocking collectives: 84.5 us -> none
    ppermute x24 -> x0, starting transfers between devices: 61.7 us -> none  [shifted(): return lax.ppermute(block, axis, route)]
    all_gather x4 -> x0, blocking collectives: 57.3 us -> none  [the longest x1 23.7 us: per_device(): lax.all_gather(head_class.astype(jnp.bfloat16), 'dp', axis=0, tiled=True)]
    psum x2 -> x0, blocking collectives: 55.3 us -> none  [the longest x1 41 us: per_device(): lax.psum((rows_class, rows_boxes, grad_hbias_class, grad_hbias_boxes), ('...]
  transfers between devices with their start and end apart: 33 -> 0, of which waited for: 11 -> 0; matrix products, arithmetic and copies ran while one was open for 36% -> 0% of each run, Pallas kernels for 0% -> 0%
where the time goes in v1:
time: 154 us; the launch traced here: 153 us
  Pallas kernels  136 us (88%)
  local copies, waits for them, and re-layouts  14.1 us (9%)
    pallas_call x1, Pallas kernels, fast(): pl.pallas_call(head_kernel, out_shape=(out((tiles, 64, CH), BF16), out((1...  136 us
    unnamed x15, local copies, waits for them, and re-layouts  8.31 us

profile of v1, /device:TPU:0, one launch (start us, length us, event | category | flops | bytes accessed | tf_op | source)
XLA Modules:
  0.0 152.6 jit_solution(4288313056834609499)
XLA Ops:
  0.6 0.0 copy-start.2
  0.7 0.1 pad.31.clone
  0.7 0.7 reshape.65
  1.5 0.8 reshape.62
  2.3 0.1 reshape.64
  2.4 0.8 fusion.3
  3.2 0.6 pad_maximum_fusion.bias
  3.8 1.5 copy.28.head_boxes
  5.3 0.0 copy-done.2
  5.3 0.9 copy.27.head_class
  6.2 136.4 %shard_map.241 = (bf16[4,64,256]{2,1,0:T(8,128)(2,1)}, f32[1,288,256]{2,1,0:T(8,128)}, f32[1,288,256]{2,1,0:T(8,128)}, f32[288,180]{1,0:T(8,128)}, f32[288,9]{1,0:T(8,128)}, /*index=5*/f32[2,8,768]{2,1,0:T(8,128)}) custom-call(bf16[4,64,256]{2,1,0:T(8,128)(2,1)} %bitcast.18, f32[1,288,256]{2,1,0:T(8,128)} %tower_class.1, f32[1,288,256]{2,1,0:T(8,128)} %tower_boxes.1, ...), custom_call_target="tpu_custom_call" | custom-call | tf_op jit(solution)/shard_map/pallas_call | solution.py:633
  142.6 0.7 slice_reduce_fusion
  143.3 0.1 reshape.69
  143.4 0.7 fusion.4
  144.1 1.3 slice_bitcast_fusion
  145.4 0.6 reshape.72
  146.0 0.7 reshape.70
  146.7 1.6 %copy.30 = f32[288,9]{0,1:T(8,128)} copy(f32[288,9]{1,0:T(8,128)} %get-tuple-element.28) | data formatting | bytes 20736
  148.3 0.0 copy-start.3
  148.3 0.0 copy-start.1
  148.3 1.9 %copy.29 = f32[288,180]{0,1:T(8,128)} copy(f32[288,180]{1,0:T(8,128)} %get-tuple-element.26) | data formatting | bytes 414720
  150.2 0.0 copy-done.3
  150.2 0.7 copy.34
  150.8 0.0 copy-done.1
  150.8 0.0 copy-start
  150.8 0.7 copy.35
  151.6 0.4 copy-done
  151.9 0.7 copy.36
  (10 shorter events, 0.1 us)
Async XLA Ops:
  0.6 4.7 %copy-start.2 = (f32[288,180]{0,1:T(8,128)S(1)}, f32[288,180]{0,1:T(8,128)}, u32[]{:S(2)}) copy-start(f32[288,180]{0,1:T(8,128)} %param.23) | copy-start | bytes 622084
  148.3 1.9 %copy-start.3 = (bf16[4,64,256]{2,1,0:T(8,128)(2,1)S(1)}, bf16[4,64,256]{2,1,0:T(8,128)(2,1)}, u32[]{:S(2)}) copy-start(bf16[4,64,256]{2,1,0:T(8,128)(2,1)} %get-tuple-element.15) | copy-start | bytes 393220
  148.3 2.5 %copy-start.1 = (f32[1,288,256]{2,1,0:T(8,128)S(1)}, f32[1,288,256]{2,1,0:T(8,128)}, u32[]{:S(2)}) copy-start(f32[1,288,256]{2,1,0:T(8,128)} %get-tuple-element.46) | copy-start | bytes 884740
  150.8 1.1 copy-start

commit v2 on v1

--- a/solution.py
+++ b/solution.py
@@ -34,7 +34,8 @@
 PACK = ROWS + HALF
 LANES = 128
 TAIL = 64
-HEAD = SECTIONS * (LANES + TAIL)
+MAIN = SECTIONS * LANES
+HEAD = MAIN + SECTIONS * TAIL
 LAB = 256
 TGT = 640
 DEEP = 9 * CH
@@ -55,7 +56,7 @@
 def constants(class_width, boxes_width):
     classes, boxes = head_layout(class_width), head_layout(boxes_width)
     spread = np.zeros((2, LAB, HEAD), np.float32)
-    targets = np.zeros((TGT, HEAD), np.float32)
+    targets = np.zeros((TGT, MAIN), np.float32)
     for j in range(TILE):
         for col in range(HEAD):
             if classes[col] >= 0:
@@ -79,11 +80,18 @@
     return lax.dot_general(a, b, (((1,), (1,)), ((), ())), preferred_element_type=F32)
 
 
+def moved_right(v):
+    col = lax.broadcasted_iota(jnp.int32, v.shape, 0) % TILE
+    return jnp.where(col == 0, 0.0, pltpu.roll(v, 1, 0))
+
+
+def moved_left(v):
+    col = lax.broadcasted_iota(jnp.int32, v.shape, 0) % TILE
+    return jnp.where(col == TILE - 1, 0.0, pltpu.roll(v, PX - 1, 0))
+
+
 def put_shifted(ref, t, v, order, width):
-    col = lax.broadcasted_iota(jnp.int32, v.shape, 0) % TILE
-    before = jnp.where(col == 0, 0.0, pltpu.roll(v, 1, 0))
-    after = jnp.where(col == TILE - 1, 0.0, pltpu.roll(v, PX - 1, 0))
-    blocks = (before, v, after) if order > 0 else (after, v, before)
+    blocks = (moved_right(v), v, moved_left(v))[::order]
     for s, block in enumerate(blocks):
         ref[t, TILE : TILE + PX, s * width : (s + 1) * width] = block.astype(BF16)
 
@@ -101,7 +109,7 @@
 
 def forward_layer(m, l):
     z = sum(dot(shifted_rows(m.act3, r), m.w[l, 3 * CH * r : 3 * CH * (r + 1), :]) for r in range(3))
-    z = z + m.bias[m.role, l : l + 1, 0:CH]
+    z = z + m.bias[l : l + 1, 0:CH]
     for t in range(2):
         zt = z[t * PX : (t + 1) * PX]
         square = zt * zt
@@ -112,11 +120,15 @@
             1.0 + (3 * 0.044715) * square
         )
         put_shifted(m.act3, t, a, 1, CH)
-        m.act_t[l + 1, :, t * PX : (t + 1) * PX] = a.T.astype(BF16)
-
-
-def head_forward(m):
-    for n in range(0, HEAD, 256):
+        if l + 1 < LAYERS:
+            m.act_t[l + 1, :, t * PX : (t + 1) * PX] = a.T.astype(BF16)
+        else:
+            for i, moved in enumerate((moved_right(a), a, moved_left(a))):
+                m.last_t[i, :, t * PX : (t + 1) * PX] = moved.T.astype(BF16)
+
+
+def head_forward(m, lanes):
+    for n in range(lanes.start, lanes.stop, 256):
         m.logits[:, n : n + 256] = sum(
             dot(shifted_rows(m.act3, r), m.wh[3 * CH * r : 3 * CH * (r + 1), n : n + 256]) for r in range(3)
         )
@@ -130,7 +142,7 @@
 def prepare_loss(m):
     for t, lab in enumerate((m.lab, m.lab_in)):
         codes = expand(lab[:, 0:LAB], m.mask_lab).astype(BF16)
-        m.code[t * PX : (t + 1) * PX, :] = dot(codes, m.spread[m.role])
+        m.code[t * PX : (t + 1) * PX, :] = dot(codes, m.spread[...])
 
     @pl.when(m.role == 1)
     def _():
@@ -141,52 +153,70 @@
             )
 
 
-def loss_gradient(m):
+def loss_gradient(m, lanes):
     total = m.count_sum[0:1, :] + m.count_in[1, 0:1, :] + m.count_in[2, 0:1, :] + m.count_in[3, 0:1, :]
-    scale = jnp.concatenate([1.0 / jnp.maximum(total, 1.0)] * (HEAD // LANES), axis=1)
-    bias = m.bias[m.role, 4:5, :]
+    width = lanes.stop - lanes.start
+    scale = jnp.concatenate([1.0 / jnp.maximum(total, 1.0)] * (width // LANES), axis=1)
+    bias = m.bias[4:5, lanes]
 
     def keep(t, g):
-        g = g.astype(BF16).astype(F32)
-        m.grad_bias[4:5, :] += jnp.sum(g, axis=0, keepdims=True)
-        put_shifted(m.g3h, t, g, -1, HEAD)
+        g = g.astype(BF16)
+        m.grad_bias[4:5, lanes] += jnp.sum(g.astype(F32), axis=0, keepdims=True)
+        m.gl[t, TILE : TILE + PX, lanes] = g
 
     @pl.when(m.role == 0)
     def _():
         for t in range(2):
             at = slice(t * PX, (t + 1) * PX)
-            x = m.logits[at, :] + bias
-            code = m.code[at, :]
-            labeled = code == m.label[0:1, :]
+            x = m.logits[at, lanes] + bias
+            code = m.code[at, lanes]
+            labeled = code == m.label[0:1, lanes]
             y = jnp.where(labeled, -x, x)
             e = jnp.exp(-jnp.abs(y))
-            q = jnp.where(y >= 0, 1.0, e) / (1.0 + e)
-            softplus = jnp.maximum(y, 0.0) + jnp.log1p(e)
+            more = 1.0 + e
+            q = jnp.where(y >= 0, 1.0, e) / more
+            softplus = jnp.maximum(y, 0.0) + jnp.log(more)
             slope = q * q * (2.0 * (1.0 - q) * softplus + q)
-            keep(t, slope * jnp.where(labeled, -0.25, jnp.where(code > 0.5, 0.75, 0.0)) * scale)
+            keep(t, slope * (jnp.where(labeled, -0.25, jnp.where(code > 0.5, 0.75, 0.0)) * scale))
 
     @pl.when(m.role == 1)
     def _():
         for t in range(2):
             at = slice(t * PX, (t + 1) * PX)
-            offset = m.logits[at, :] + bias - m.target[at, :]
-            keep(t, jnp.where(m.code[at, :] > 1.5, jnp.clip(offset / huber_beta, -1.0, 1.0), 0.0) * scale)
-
-
-def head_kernel_gradient(m, r):
+            if lanes.start < MAIN:
+                offset = m.logits[at, lanes] + bias - m.target[at, lanes]
+                g = jnp.where(m.code[at, lanes] > 1.5, jnp.clip(offset / huber_beta, -1.0, 1.0), 0.0)
+                keep(t, g * scale)
+            else:
+                m.gl[t, TILE : TILE + PX, lanes] = jnp.zeros((PX, width), BF16)
+
+
+def head_kernel_gradient(m, lanes, r):
     for s in range(3):
         at = (3 * r + s) * CH
-        m.gh[at : at + CH, :] = dot(
-            m.act_t[LAYERS], shifted_rows(m.g3h, 2 - r, slice(s * HEAD, (s + 1) * HEAD))
-        ).astype(BF16)
-
-
-def input_gradient(m, g3, width, kernel):
+        m.gh[at : at + CH, lanes] = dot(m.last_t[s], shifted_rows(m.gl, 2 - r, lanes)).astype(BF16)
+
+
+def head_input_gradient(m):
+    columns = []
+    for s in range(3):
+        acc = None
+        for r in range(3):
+            at = (3 * r + s) * CH
+            part = dot_nt(shifted_rows(m.gl, 2 - r), m.wh[at : at + CH, :])
+            acc = part if acc is None else acc + part
+        columns.append(acc)
+    for t in range(2):
+        at = slice(t * PX, (t + 1) * PX)
+        m.da[at, :] = moved_left(columns[0][at]) + columns[1][at] + moved_right(columns[2][at])
+
+
+def input_gradient(m, g3, kernel):
     acc = None
     for r in range(3):
         for s in range(3):
             at = (3 * r + s) * CH
-            part = dot_nt(shifted_rows(g3, 2 - r, slice(s * width, (s + 1) * width)), kernel[at : at + CH, :])
+            part = dot_nt(shifted_rows(g3, 2 - r, slice(s * CH, (s + 1) * CH)), kernel[at : at + CH, :])
             acc = part if acc is None else acc + part
     return acc
 
@@ -239,17 +269,27 @@
 
 
 SEMAPHORES = 192
-GATHER_ORDER = (
-    ("T", 0, "A"), ("H", 0, "B"), ("T", 1, "B"), ("T", 3, "A"), ("T", 2, "B"), ("H", 1, "A"), ("H", 3, "B"), ("H", 2, "A"),
+WAYS = {
+    "T0": "A", "T1": "B", "T3": "A", "T2": "B", "M0": "B", "M1": "A", "M3": "B", "M2": "A", "U0": "A", "U1": "B", "U3": "A", "U2": "B",
+}
+SCHEDULE = (
+    "aT0", "zT", "f", "aM0", "aT1", "bM0", "bT0", "zM", "e", "bT1", "aT3", "aT2", "cT1", "zU", "cM0", "bT3", "bT2",
+    "aM2", "aM1", "aU0", "cT0", "aM3", "y", "aU1", "cT3", "cT2", "F0", "bM2", "F1", "bM3", "bM1", "aU2", "F2",
+    "cM2", "bU0", "aU3", "F3", "cM1", "cM3", "bU2", "bU1", "cU0", "bU3", "HM", "cU3", "WM0", "WM1", "WM2", "cU2",
+    "kM0", "cU1", "kM2", "kM3", "kM1", "HU", "X", "u3", "pM0", "pM3", "w3", "x3", "k3", "u2", "pM2", "w2", "pM1",
+    "x2", "k2", "qM0", "u1", "x1", "w1", "qM2", "qM1", "p3", "u0", "WU0", "qM3", "WU1", "k1", "WU2", "w0", "p2",
+    "k0", "q3", "p1", "x0", "kU2", "q2", "s3", "p0", "kU3", "Bk", "q1", "kU1", "kU0", "q0", "Bp", "D", "pU3", "s2",
+    "pU0", "sM", "pU1", "Bq", "s1", "E", "pU2", "qU0", "s0", "qU3", "qU1", "qU2", "Bs", "t", "sU",
 )
 
 
 def head_kernel(
-    features, tower_class, tower_boxes, head_class, head_boxes, bias, state, labels, targets_in, valid,
-    spread, targets, mask_lab, mask_tgt, label,
-    out_features, out_class, out_boxes, out_head_class, out_head_boxes, out_bias,
-    own, own_h, w, wh, hp, g, gh, rc, rch, sh, r1, r1h, r2, r2h, rz, rzh,
-    act3, g3, g3h, act_t, slope, logits, code, target, da,
+    features, tower_class, tower_boxes, head_class, head_boxes, bias_class, bias_boxes, head_class_bias, head_boxes_bias,
+    state, labels, targets_in, valid, label, spread_any, targets_any, mask_lab_any, mask_tgt_any,
+    out_features, out_towers, out_heads, out_bias,
+    spread, targets, mask_lab, mask_tgt, bias, fetch_sem,
+    own, own_h, w, wh, hp, g, gh, rc, rch, sm, su, r1a, r1b, r1m, r1u, r2, r2m, r2u, quarter, sum_m, sum_u, rz, rzm, rzu, done, layer_in,
+    act3, g3, gl, act_t, last_t, slope, logits, code, target, da,
     x, lab, lab_in, count_mine, count_sum, count_in, grad_bias, bias_in, bias_z, dx, dx_in, tile_out, features_in,
     send_sem, recv_sem,
 ):
@@ -263,7 +303,7 @@
     role = my_z % 2
     net = Traffic(send_sem, recv_sem)
     m = SimpleNamespace(
-        w=w, wh=wh, g=g, gh=gh, act3=act3, g3=g3, g3h=g3h, act_t=act_t, slope=slope, logits=logits, code=code,
+        w=w, wh=wh, g=g, gh=gh, act3=act3, g3=g3, gl=gl, act_t=act_t, last_t=last_t, slope=slope, logits=logits, code=code,
         target=target, da=da, lab=lab, lab_in=lab_in, count_sum=count_sum, count_in=count_in, grad_bias=grad_bias,
         bias=bias, spread=spread, targets=targets, mask_lab=mask_lab, mask_tgt=mask_tgt, label=label, role=role,
     )
@@ -276,15 +316,24 @@
     for peer in peers:
         pl.semaphore_signal(barrier, inc=1, device_id=peer, device_id_type=MESH)
 
+    constants_in = [
+        pltpu.make_async_copy(src, dst, fetch_sem.at[i])
+        for i, (src, dst) in enumerate(
+            ((mask_lab_any, mask_lab), (spread_any.at[role], spread), (mask_tgt_any, mask_tgt), (targets_any, targets))
+        )
+    ]
+    for copy in constants_in:
+        copy.start()
+
     for role_at, (tower, head) in enumerate(((tower_class, head_class), (tower_boxes, head_boxes))):
         own[role_at] = tower[0].astype(BF16)
-        width = head.shape[1]
+        width = head.shape[0]
         main = min(width, LANES)
         own_h[role_at] = jnp.zeros((PACK, LANES), BF16)
-        own_h[role_at, 0:ROWS, 0:main] = head[:, 0:main].astype(BF16)
+        own_h[role_at, 0:ROWS, 0:main] = head[0:main, :].T.astype(BF16)
         if width > LANES:
             logits[0:ROWS, 0:LANES] = jnp.zeros((ROWS, LANES), F32)
-            logits[0:ROWS, 0 : width - LANES] = head[:, LANES:width]
+            logits[0:ROWS, 0 : width - LANES] = head[LANES:width, :].T
             own_h[role_at, ROWS:PACK, :] = (
                 logits[0:HALF, 0:LANES] + pltpu.roll(logits[HALF:ROWS, 0:LANES], TAIL, 1)
             ).astype(BF16)
@@ -306,81 +355,98 @@
 
     pl.semaphore_wait(barrier, len(peers))
 
-    for kind_name, src, dst in (("T", own, w), ("H", own_h, hp)):
+    def head_lanes(sec):
+        return pl.ds(pl.multiple_of(LANES * sec, LANES), LANES)
+
+    def place(kind_name, sec, z):
+        if kind_name == "T":
+            return w.at[sec, shard(z, my_c), :]
+        if kind_name == "M":
+            return wh.at[shard(z, my_c), head_lanes(sec)]
+        return hp.at[sec, z]
+
+    def own_shard(kind_name, which):
+        if kind_name == "T":
+            return own.at[which]
+        return own_h.at[which, pl.ds(0, ROWS) if kind_name == "M" else pl.ds(ROWS, HALF), :]
+
+    def planes_send(kind_name):
         for k in (1, 3, 2):
-            at = dst.at[s, shard(my_z, my_c), :] if kind_name == "T" else dst.at[s, my_z]
-            net.send(("z", kind_name, k), src.at[plane(k) % 2], at, to_z(k))
-        if kind_name == "T":
-            for name, peer, sec in (("x", to_x, sx), ("y", to_y, sy), ("g", to_g, sg)):
-                net.send(("f", name), features.at[sec], x.at[0, pl.ds(pl.multiple_of(64 * s, 64), 64), :], peer)
-            net.send("count c", count_mine, count_in.at[0], to_c)
-            net.send("lab", lab, lab_in, to_pair)
-    w[s, shard(my_z, my_c), :] = own[role]
-    hp[s, my_z] = own_h[role]
+            net.send(
+                ("z", kind_name, k), own_shard(kind_name, plane(k) % 2), place(kind_name, s, my_z), to_z(k)
+            )
+
+    in_plane = (("x", to_x, sx), ("y", to_y, sy), ("g", to_g, sg))
+
+    def rows_of(sec):
+        return pl.ds(pl.multiple_of(64 * sec, 64), 64)
+
+    def features_send():
+        for name, peer, sec in in_plane:
+            net.send(("f", name), features.at[sec], x.at[0, rows_of(s), :], peer)
+        net.send("count c", count_mine, count_in.at[0], to_c)
+        net.send("lab", lab, lab_in, to_pair)
 
     def piece(kind_name, sec, j):
-        z = (my_z + PLANES - j) % PLANES
-        return w.at[sec, shard(z, my_c), :] if kind_name == "T" else hp.at[sec, z]
-
-    def ways(way):
-        return ((to_x, sx), (to_y, sy)) if way == "A" else ((to_y, sy), (to_x, sx))
-
-    def gather_first(kind_name, j, way):
-        (n1, s1), (n2, s2) = ways(way)
+        return place(kind_name, sec, (my_z + PLANES - j) % PLANES)
+
+    def ways(kind_name, j):
+        if WAYS[kind_name + str(j)] == "A":
+            return (to_x, sx), (to_y, sy)
+        return (to_y, sy), (to_x, sx)
+
+    def gather_mine(kind_name, j):
+        mine = piece(kind_name, s, j)
         if j:
-            net.arrived(("z", kind_name, j), piece(kind_name, s, j), to_z(PLANES - j))
-        mine = piece(kind_name, s, j)
-        net.send(("g1", kind_name, j), mine, mine, n1)
+            net.arrived(("z", kind_name, j), mine, to_z(PLANES - j))
+        for (n, _), name in zip(ways(kind_name, j), ("g1", "g2")):
+            net.send((name, kind_name, j), mine, mine, n)
         if kind_name == "T":
             net.send(("swap", kind_name, j, 0), mine, mine, to_c)
 
-    def gather_second(kind_name, j, way):
-        (n1, s1), (n2, s2) = ways(way)
-        mine, first = piece(kind_name, s, j), piece(kind_name, s1, j)
-        net.send(("g2", kind_name, j), mine, mine, n2)
+    def gather_pass(kind_name, j):
+        (n1, s1), (n2, s2) = ways(kind_name, j)
+        first = piece(kind_name, s1, j)
         net.arrived(("g1", kind_name, j), first, n1)
         net.send(("g3", kind_name, j), first, first, n2)
         if kind_name == "T":
             net.send(("swap", kind_name, j, 1), first, first, to_c)
 
-    def gather_third(kind_name, j, way):
-        (n1, s1), (n2, s2) = ways(way)
+    def gather_last(kind_name, j):
+        (n1, s1), (n2, s2) = ways(kind_name, j)
         for i, (name, sec) in enumerate((("g2", s2), ("g3", sg))):
             got = piece(kind_name, sec, j)
             net.arrived((name, kind_name, j), got, n2)
             if kind_name == "T":
                 net.send(("swap", kind_name, j, 2 + i), got, got, to_c)
-        if kind_name == "H":
-            z = (my_z + PLANES - j) % PLANES
-            at = pl.multiple_of(ROWS * (2 * z + my_c), 16)
-            for sec in range(SECTIONS):
-                wh[pl.ds(at, ROWS), sec * LANES : (sec + 1) * LANES] = hp[sec, z, 0:ROWS, :]
+        z = (my_z + PLANES - j) % PLANES
+        at = pl.multiple_of(ROWS * (2 * z + my_c), 16)
+        if kind_name == "M":
+            block = wh.at[pl.ds(at, ROWS), 0:MAIN]
+            net.send(("swap", "M", j), block, block, to_c)
+        if kind_name == "U":
             for q in range(2):
                 lanes = slice((SECTIONS + q) * LANES, (SECTIONS + q + 1) * LANES)
-                top, bottom = swap_halves(hp[2 * q, z, ROWS:PACK, :], hp[2 * q + 1, z, ROWS:PACK, :])
+                top, bottom = swap_halves(hp[2 * q, z], hp[2 * q + 1, z])
                 wh[pl.ds(at, HALF), lanes] = top.astype(BF16)
                 wh[pl.ds(at + HALF, HALF), lanes] = bottom.astype(BF16)
-            block = wh.at[pl.ds(at, ROWS), :]
-            net.send(("swap", "H", j), block, block, to_c)
+            block = wh.at[pl.ds(at, ROWS), MAIN:HEAD]
+            net.send(("swap", "U", j), block, block, to_c)
 
     def swapped(kind_name, j):
         z = (my_z + PLANES - j) % PLANES
-        if kind_name == "H":
-            net.arrived(("swap", "H", j), wh.at[shard(z, 1 - my_c), :], to_c)
+        if kind_name != "T":
+            lanes = slice(0, MAIN) if kind_name == "M" else slice(MAIN, HEAD)
+            net.arrived(("swap", kind_name, j), wh.at[shard(z, 1 - my_c), lanes], to_c)
             return
-        (_, s1), (_, s2) = ways(dict((entry[:2], entry[2]) for entry in GATHER_ORDER)[(kind_name, j)])
+        (_, s1), (_, s2) = ways(kind_name, j)
         for i, sec in enumerate((s, s1, s2, sg)):
             net.arrived(("swap", "T", j, i), w.at[sec, shard(z, 1 - my_c), :], to_c)
 
-    def start():
-        for ref in (act3, g3, g3h):
-            for t in range(2):
-                ref[t, 0:TILE, :] = jnp.zeros((TILE, ref.shape[2]), BF16)
-                ref[t, TILE + PX : 2 * TILE + PX, :] = jnp.zeros((TILE, ref.shape[2]), BF16)
-        grad_bias[...] = jnp.zeros_like(grad_bias)
-        x[0, pl.ds(pl.multiple_of(64 * s, 64), 64), :] = features[s]
-        for name, peer, sec in (("x", to_x, sx), ("y", to_y, sy), ("g", to_g, sg)):
-            net.arrived(("f", name), x.at[0, pl.ds(pl.multiple_of(64 * sec, 64), 64), :], peer)
+    def features_tile():
+        x[0, rows_of(s), :] = features[s]
+        for name, peer, sec in in_plane:
+            net.arrived(("f", name), x.at[0, rows_of(sec), :], peer)
         net.send("tile", x.at[0], x.at[1], to_pair)
         net.arrived("count c", count_in.at[0], to_c)
         count_sum[...] = count_mine[...] + count_in[0]
@@ -388,6 +454,15 @@
             net.send(("count", k), count_sum, count_in.at[k], to_z(k))
 
     def prepare():
+        for ref in (act3, g3, gl):
+            for t in range(2):
+                ref[t, 0:TILE, :] = jnp.zeros((TILE, ref.shape[2]), BF16)
+                ref[t, TILE + PX : 2 * TILE + PX, :] = jnp.zeros((TILE, ref.shape[2]), BF16)
+        grad_bias[...] = jnp.zeros_like(grad_bias)
+        for copy in constants_in:
+            copy.wait()
+        bias[0:LAYERS, 0:CH] = jnp.where(role == 0, bias_class[...], bias_boxes[...])
+        bias[4:5, :] = jnp.where(role == 0, lay(head_class_bias[...]), lay(head_boxes_bias[...]))
         net.arrived("lab", lab_in, to_pair)
         prepare_loss(m)
         net.arrived("tile", x.at[1], to_pair)
@@ -396,277 +471,338 @@
             put_shifted(act3, t, v, 1, CH)
             act_t[0, :, t * PX : (t + 1) * PX] = v.T.astype(BF16)
 
-    stages = len(GATHER_ORDER) + 2
-    towers_done = max(i for i, entry in enumerate(GATHER_ORDER) if entry[0] == "T") + 2
-    for i in range(stages):
-        if i < len(GATHER_ORDER):
-            gather_first(*GATHER_ORDER[i])
-        if 1 <= i < len(GATHER_ORDER) + 1:
-            gather_second(*GATHER_ORDER[i - 1])
-        if i >= 2:
-            gather_third(*GATHER_ORDER[i - 2])
-        if i == 1:
-            start()
-        if i == 2:
-            prepare()
-        if i == towers_done:
+    def forward(l):
+        if l == 0:
             for j in range(PLANES):
                 swapped("T", j)
-        if towers_done <= i < towers_done + LAYERS:
-            forward_layer(m, i - towers_done)
-    for l in range(max(0, stages - towers_done), LAYERS):
         forward_layer(m, l)
-    for k in (1, 2, 3):
-        net.arrived(("count", k), count_in.at[k], to_z(PLANES - k))
-    for j in range(PLANES):
-        swapped("H", j)
-
-    def summed(refs_into, refs_from):
-        refs_into[...] = (refs_into[...].astype(F32) + refs_from[...].astype(F32)).astype(BF16)
-
-    def reduce_start(l, zp):
-        if l is None:
-            net.send(("rc", l, zp), gh.at[shard(zp, 1 - my_c), :], rch.at[zp], to_c)
+
+    def head(kind_name):
+        if kind_name == "M":
+            for k in (1, 2, 3):
+                net.arrived(("count", k), count_in.at[k], to_z(PLANES - k))
+        for j in range(PLANES):
+            swapped(kind_name, j)
+        head_forward(m, head_part[kind_name])
+        loss_gradient(m, head_part[kind_name])
+
+    head_part = dict(M=slice(0, MAIN), U=slice(MAIN, HEAD))
+    w[s, shard(my_z, my_c), :] = own[role]
+    wh[shard(my_z, my_c), head_lanes(s)] = own_h[role, 0:ROWS, :]
+    hp[s, my_z] = own_h[role, ROWS:PACK, :]
+
+    def added(*values):
+        return sum(v.astype(F32) for v in values).astype(BF16)
+
+    def half_rows(which):
+        return pl.ds(pl.multiple_of(HALF * which, 16), HALF)
+
+    def half_lanes(which):
+        return pl.ds(pl.multiple_of(LANES * which, LANES), LANES)
+
+    def core_send(l, zp):
+        theirs = shard(zp, 1 - my_c)
+        if l in head_part:
+            net.send(("rc", l, zp), gh.at[theirs, head_part[l]], rch.at[zp, :, head_part[l]], to_c)
         else:
-            net.send(("rc", l, zp), g.at[l, shard(zp, 1 - my_c), :], rc.at[l, zp], to_c)
-
-    def bound(l, zp):
-        x_here, y_here = my_x == l % 2, my_y == l // 2
-        if zp < 2:
-            return x_here, y_here, to_x, to_y
-        return y_here, x_here, to_y, to_x
-
-    def buffers(kind_name, l, zp):
-        if kind_name == "T":
-            return rc.at[l, zp], r1.at[l, zp], r2.at[zp]
-        return sh.at[l, zp], r1h.at[l, zp], r2h.at[zp]
-
-    def reduce_first_send(kind_name, l, zp):
-        here1, here2, n1, n2 = bound(l, zp)
-        mine, into1, into2 = buffers(kind_name, l, zp)
-        away = jnp.logical_not(here1)
-
-        net.send(("r1", kind_name, l, zp), mine, into1, n1, away)
-
-    def reduce_cores_tower(l, zp):
-        net.arrived(("rc", l, zp), rc.at[l, zp], to_c)
-        rc[l, zp] = (rc[l, zp].astype(F32) + g[l, shard(zp, my_c), :].astype(F32)).astype(BF16)
-        reduce_first_send("T", l, zp)
-
-    def reduce_cores_head(zp):
-        net.arrived(("rc", None, zp), rch.at[zp], to_c)
-        at = pl.multiple_of(ROWS * (2 * zp + my_c), 16)
-        for sec in range(SECTIONS):
-            lanes = slice(sec * LANES, (sec + 1) * LANES)
-            sh[sec, zp, 0:ROWS, :] = (
-                rch[zp, :, lanes].astype(F32) + gh[pl.ds(at, ROWS), lanes].astype(F32)
-            ).astype(BF16)
-        for q in range(2):
-            lanes = slice((SECTIONS + q) * LANES, (SECTIONS + q + 1) * LANES)
-            top = rch[zp, 0:HALF, lanes].astype(F32) + gh[pl.ds(at, HALF), lanes].astype(F32)
-            bottom = rch[zp, HALF:ROWS, lanes].astype(F32) + gh[pl.ds(at + HALF, HALF), lanes].astype(F32)
-            first, second = swap_halves(top, bottom)
-            sh[2 * q, zp, ROWS:PACK, :] = first.astype(BF16)
-            sh[2 * q + 1, zp, ROWS:PACK, :] = second.astype(BF16)
-        for sec in range(SECTIONS):
-            reduce_first_send("H", sec, zp)
-
-    def reduce_second(kind_name, l, zp):
-        here1, here2, n1, n2 = bound(l, zp)
-        mine, into1, into2 = buffers(kind_name, l, zp)
-
-        @pl.when(here1)
-        def _():
-            net.arrived(("r1", kind_name, l, zp), into1, n1)
-            summed(mine, into1)
-
-        away = jnp.logical_and(here1, jnp.logical_not(here2))
-
-        net.send(("r2", kind_name, zp), mine, into2, n2, away)
-
-    def reduce_third(kind_name, l, zp):
-        here1, here2, n1, n2 = bound(l, zp)
-        mine, into1, into2 = buffers(kind_name, l, zp)
+            net.send(("rc", l, zp), g.at[l, theirs, :], rc.at[l, zp], to_c)
+
+    first, second = pl.ds(0, 2), pl.ds(2, 2)
+
+    def tower_cores(l):
+        for zp in range(PLANES):
+            net.arrived(("rc", l, zp), rc.at[l, zp], to_c)
+            rc[l, zp] = added(rc[l, zp], g[l, shard(zp, my_c), :])
+            if zp == 1:
+                net.send(("r1a", l), rc.at[l, first, :, half_lanes(1 - my_x)], r1a.at[l], to_x)
+        net.send(("r1b", l), rc.at[l, second, half_rows(1 - my_y), :], r1b.at[l], to_y)
+
+    def tower_plane(l):
+        net.arrived(("r1a", l), r1a.at[l], to_x)
+        for zp in (0, 1):
+            rc[l, zp, :, half_lanes(my_x)] = added(rc[l, zp, :, half_lanes(my_x)], r1a[l, zp])
+        net.send(("r2a", l), rc.at[l, first, half_rows(1 - my_y), half_lanes(my_x)], r2.at[l, first], to_y)
+        net.arrived(("r1b", l), r1b.at[l], to_y)
+        for zp in (2, 3):
+            rc[l, zp, half_rows(my_y), :] = added(rc[l, zp, half_rows(my_y), :], r1b[l, zp - 2])
+        net.send(("r2b", l), rc.at[l, second, half_rows(my_y), half_lanes(1 - my_x)], r2.at[l, second], to_x)
+
+    def to_planes(name, src, dst):
+        for zp in range(PLANES):
+            k = (zp + PLANES - my_z) % PLANES
+            net.send(name, src.at[zp], dst.at[my_z], (s, 2 * zp + my_c), my_z != zp, span=PLANES, offset=k)
+
+    def tower_planes(l):
+        net.arrived(("r2a", l), r2.at[l, first], to_y)
+        net.arrived(("r2b", l), r2.at[l, second], to_x)
+        for zp in range(PLANES):
+            quarter[l, zp] = added(rc[l, zp, half_rows(my_y), half_lanes(my_x)], r2[l, zp])
+        to_planes(("rz", l), quarter.at[l], rz.at[l])
+
+    def from_planes(name, mine, others):
+        for k in (1, 2, 3):
+            net.arrived(name, others.at[plane(PLANES - k)], to_z(PLANES - k), span=PLANES, offset=k)
+        same = mine[my_z].astype(F32) + others[plane(2)].astype(F32)
+        return same, others[plane(1)].astype(F32) + others[plane(3)].astype(F32)
+
+    def tower_sum(l):
+        same, other = from_planes(("rz", l), quarter.at[l], rz.at[l])
+        done[l, role] = same.astype(BF16)
+        done[l, 1 - role] = other.astype(BF16)
+        to_l = (l, dp)
+        net.send("layer", done.at[l], layer_in.at[s], to_l, s != l, span=SECTIONS, offset=s)
 
         @pl.when(s == l)
         def _():
-            net.arrived(("r2", kind_name, zp), into2, n2)
-            summed(mine, into2)
-
-        away = jnp.logical_and(s == l, my_z != zp)
-        out = rz if kind_name == "T" else rzh
+            out_towers[role, half_rows(my_y), half_lanes(my_x)] = same
+            out_towers[1 - role, half_rows(my_y), half_lanes(my_x)] = other
+
+    def tower_store():
+        for sec, peer in ((sx, to_x), (sy, to_y), (sg, to_g)):
+            net.arrived("layer", layer_in.at[sec], peer, span=SECTIONS, offset=sec)
+            for i in range(2):
+                out_towers[i, half_rows(sec // 2), half_lanes(sec % 2)] = layer_in[sec, i].astype(F32)
+
+    def head_refs(kind_name):
+        return (sm, r1m, r2m, sum_m, rzm) if kind_name == "M" else (su, r1u, r2u, sum_u, rzu)
+
+    def head_cores(kind_name, zp):
+        lanes = head_part[kind_name]
+        net.arrived(("rc", kind_name, zp), rch.at[zp, :, lanes], to_c)
+        at = pl.multiple_of(ROWS * (2 * zp + my_c), 16)
+        into, landing = head_refs(kind_name)[:2]
+        if kind_name == "M":
+            for sec in range(SECTIONS):
+                lanes = slice(sec * LANES, (sec + 1) * LANES)
+                into[sec // 2, sec % 2, zp] = added(rch[zp, :, lanes], gh[pl.ds(at, ROWS), lanes])
+        else:
+            for q in range(2):
+                lanes = slice((SECTIONS + q) * LANES, (SECTIONS + q + 1) * LANES)
+                top = rch[zp, 0:HALF, lanes].astype(F32) + gh[pl.ds(at, HALF), lanes].astype(F32)
+                bottom = rch[zp, HALF:ROWS, lanes].astype(F32) + gh[pl.ds(at + HALF, HALF), lanes].astype(F32)
+                left, right = swap_halves(top, bottom)
+                into[q, 0, zp] = left.astype(BF16)
+                into[q, 1, zp] = right.astype(BF16)
+        if zp % 2 == 0:
+            net.send(("h1", kind_name, zp), into.at[:, 1 - my_x, zp], landing.at[zp], to_x)
+        else:
+            net.send(("h1", kind_name, zp), into.at[1 - my_y, :, zp], landing.at[zp], to_y)
+
+    def head_plane(kind_name, zp):
+        into, landing, landing2 = head_refs(kind_name)[:3]
+        net.arrived(("h1", kind_name, zp), landing.at[zp], to_x if zp % 2 == 0 else to_y)
+        for i in range(2):
+            at = (i, my_x, zp) if zp % 2 == 0 else (my_y, i, zp)
+            into[at] = added(into[at], landing[zp, i])
+        if zp % 2 == 0:
+            net.send(("h2", kind_name, zp), into.at[1 - my_y, my_x, zp], landing2.at[zp], to_y)
+        else:
+            net.send(("h2", kind_name, zp), into.at[my_y, 1 - my_x, zp], landing2.at[zp], to_x)
+
+    def head_planes(kind_name, zp):
+        into, _, landing2, total, others = head_refs(kind_name)
+        net.arrived(("h2", kind_name, zp), landing2.at[zp], to_y if zp % 2 == 0 else to_x)
+        total[zp] = added(into[my_y, my_x, zp], landing2[zp])
         k = (zp + PLANES - my_z) % PLANES
-        net.send(("rz", kind_name), mine, out.at[my_z], (s, 2 * zp + my_c), away, span=PLANES, offset=k)
-
-    def collect(kind_name):
-        mine, others = (rc, rz) if kind_name == "T" else (sh, rzh)
+        net.send(
+            ("hz", kind_name), total.at[zp], others.at[my_z], (s, 2 * zp + my_c), my_z != zp, span=PLANES, offset=k
+        )
+
+    def head_store(kind_name):
+        total, others = head_refs(kind_name)[3:]
+        same, other = from_planes(("hz", kind_name), total, others)
+        at = slice(0, ROWS) if kind_name == "M" else slice(ROWS, PACK)
+        out_heads[role, at] = same
+        out_heads[1 - role, at] = other
+
+    def bias_cores():
+        net.arrived("bias c", bias_in.at[0], to_c)
+        bias_z[0] = grad_bias[...] + bias_in[0]
+        net.send("bias x", bias_z.at[0], bias_in.at[1], to_x)
+
+    def bias_plane():
+        net.arrived("bias x", bias_in.at[1], to_x)
+        bias_z[1] = bias_z[0] + bias_in[1]
+        net.send("bias y", bias_z.at[1], bias_in.at[2], to_y)
+
+    def bias_planes():
+        net.arrived("bias y", bias_in.at[2], to_y)
+        bias_z[2] = bias_z[1] + bias_in[2]
         for k in (1, 2, 3):
-            source = plane(PLANES - k)
-            net.arrived(("rz", kind_name), others.at[source], to_z(PLANES - k), span=PLANES, offset=k)
-        same = mine[s, my_z].astype(F32) + others[plane(2)].astype(F32)
-        return same, others[plane(1)].astype(F32) + others[plane(3)].astype(F32)
-
-    def by_role(same, other, store):
-        @pl.when(role == 0)
-        def _():
-            store(same, other)
-
-        @pl.when(role == 1)
-        def _():
-            store(other, same)
-
-    def store_towers(of_class, of_boxes):
-        out_class[0] = of_class
-        out_boxes[0] = of_boxes
-
-    def store_heads(of_class, of_boxes):
-        for packed, out in ((of_class, out_head_class), (of_boxes, out_head_boxes)):
-            width = out.shape[1]
-            main, rest = min(width, LANES), max(0, width - LANES)
-            out[:, 0:main] = packed[0:ROWS, 0:main]
-            if rest:
-                out[0:HALF, LANES:width] = packed[ROWS:PACK, 0:rest]
-                out[HALF:ROWS, LANES:width] = pltpu.roll(packed[ROWS:PACK, :], TAIL, 1)[:, 0:rest]
-
-    head_forward(m)
-    loss_gradient(m)
-    for r in range(3):
-        head_kernel_gradient(m, r)
+            net.send(("bias z", k), bias_z.at[2], bias_in.at[2 + k], to_z(k))
+
+    def bias_store():
+        for k in (1, 2, 3):
+            net.arrived(("bias z", k), bias_in.at[2 + k], to_z(PLANES - k))
+        out_bias[role] = bias_z[2] + bias_in[4]
+        out_bias[1 - role] = bias_in[3] + bias_in[5]
+
+    def features_sum():
+        net.arrived("dx", dx_in, to_pair)
+        tile_out[...] = (da[0:PX, :] + dx_in[...].astype(F32)).astype(BF16)
+        for name, peer, sec in in_plane:
+            net.send(("b", name), tile_out.at[rows_of(sec), :], features_in.at[s], peer)
+
+    def features_store():
+        for name, peer, sec in in_plane:
+            net.arrived(("b", name), features_in.at[sec], peer)
+            out_features[sec] = features_in[sec]
+        out_features[s] = tile_out[rows_of(s), :]
+
+    def head_gradient(kind_name, r):
+        head_kernel_gradient(m, head_part[kind_name], r)
         for zp in ((0,), (1,), (2, 3))[r]:
-            reduce_start(None, zp)
-        if r:
-            reduce_cores_head(r - 1)
-    da[...] = input_gradient(m, g3h, HEAD, wh)
-    reduce_cores_head(2)
-    reduce_cores_head(3)
-    for l in range(LAYERS - 1, -1, -1):
+            core_send(kind_name, zp)
+
+    def head_input():
+        head_input_gradient(m)
+
+    def upstream(l):
         layer_upstream(m, l)
         if l == 0:
             net.send("bias c", grad_bias, bias_in.at[0], to_c)
+
+    def layer_gradient(l):
         for r in range(3):
             layer_kernel_gradient(m, l, r)
             for zp in ((0,), (1,), (2, 3))[r]:
-                reduce_start(l, zp)
-        da[...] = input_gradient(m, g3, CH, w.at[l])
+                core_send(l, zp)
+
+    def layer_input(l):
+        da[...] = input_gradient(m, g3, w.at[l])
         if l == 0:
             dx[...] = da[PX : 2 * PX, :].astype(BF16)
             net.send("dx", dx, dx_in, to_pair)
-        for zp in range(PLANES):
-            reduce_cores_tower(l, zp)
-
-    net.arrived("bias c", bias_in.at[0], to_c)
-    bias_z[0] = grad_bias[...] + bias_in[0]
-    net.send("bias x", bias_z.at[0], bias_in.at[1], to_x)
-
-    for zp in range(PLANES):
-        for sec in range(SECTIONS):
-            reduce_second("H", sec, zp)
-    net.arrived("bias x", bias_in.at[1], to_x)
-    bias_z[1] = bias_z[0] + bias_in[1]
-    net.send("bias y", bias_z.at[1], bias_in.at[2], to_y)
-
-    net.arrived("dx", dx_in, to_pair)
-    tile_out[...] = (da[0:PX, :] + dx_in[...].astype(F32)).astype(BF16)
-    mine_at = pl.ds(pl.multiple_of(64 * s, 64), 64)
-    for name, peer, sec in (("x", to_x, sx), ("y", to_y, sy), ("g", to_g, sg)):
-        net.send(
-            ("b", name), tile_out.at[pl.ds(pl.multiple_of(64 * sec, 64), 64), :], features_in.at[s], peer
-        )
-    for l in range(LAYERS - 1, -1, -1):
-        for zp in range(PLANES):
-            reduce_second("T", l, zp)
-        if l == LAYERS - 1:
-            net.arrived("bias y", bias_in.at[2], to_y)
-            bias_z[2] = bias_z[1] + bias_in[2]
-            for k in (1, 2, 3):
-                net.send(("bias z", k), bias_z.at[2], bias_in.at[2 + k], to_z(k))
-            for zp in range(PLANES):
-                for sec in range(SECTIONS):
-                    reduce_third("H", sec, zp)
-        else:
-            for zp in range(PLANES):
-                reduce_third("T", l + 1, zp)
-    for name, peer, sec in (("x", to_x, sx), ("y", to_y, sy), ("g", to_g, sg)):
-        net.arrived(("b", name), features_in.at[sec], peer)
-        out_features[sec] = features_in[sec]
-    out_features[s] = tile_out[mine_at, :]
-    for k in (1, 2, 3):
-        net.arrived(("bias z", k), bias_in.at[2 + k], to_z(PLANES - k))
-    out_bias[role] = bias_z[2] + bias_in[4]
-    out_bias[1 - role] = bias_in[3] + bias_in[5]
-    by_role(*collect("H"), store_heads)
-    for zp in range(PLANES):
-        reduce_third("T", 0, zp)
-    by_role(*collect("T"), store_towers)
+
+    def either(of_head, of_tower):
+        return lambda *which: of_head(*which) if which[0] in head_part else of_tower(*which)
+
+    steps = dict(
+        z=planes_send, f=features_send, e=features_tile, y=prepare, a=gather_mine, b=gather_pass, c=gather_last,
+        F=forward, H=head, W=head_gradient, X=head_input, u=upstream, w=layer_gradient, x=layer_input,
+        k=either(head_cores, tower_cores), p=either(head_plane, tower_plane), q=either(head_planes, tower_planes),
+        s=either(head_store, tower_sum), t=tower_store, D=features_sum, E=features_store,
+        B=lambda which: dict(k=bias_cores, p=bias_plane, q=bias_planes, s=bias_store)[which](),
+    )
+    for step in SCHEDULE:
+        steps[step[0]](*(int(v) if v.isdigit() else v for v in step[1:]))
     net.finish()
+
+
+def lay(vector):
+    width = vector.shape[0]
+    per = width // SECTIONS
+    row = jnp.concatenate([vector.reshape(1, width), jnp.zeros((1, HEAD - width), F32)], axis=1)
+    row = jnp.broadcast_to(row, (8, HEAD))
+    lane = lax.broadcasted_iota(jnp.int32, (8, LANES), 1)
+    main, tails = [], []
+    for s in range(SECTIONS):
+        turned = pltpu.roll(row, (HEAD - s * per) % HEAD, 1)
+        main.append(jnp.where(lane < per, turned[:, 0:LANES], 0.0))
+        tails.append(jnp.where(lane < per - LANES, turned[:, LANES : 2 * LANES], 0.0))
+    folded = [tails[2 * q] + pltpu.roll(tails[2 * q + 1], TAIL, 1) for q in range(2)]
+    return jnp.concatenate(main + folded, axis=1)[0:1, :]
+
+
+def unlay(row, width):
+    per = width // SECTIONS
+    row = jnp.broadcast_to(row, (8, HEAD))
+    lane = lax.broadcasted_iota(jnp.int32, (8, LANES), 1)
+    total = jnp.zeros((8, HEAD), F32)
+    for s in range(SECTIONS):
+        tail = row[:, MAIN + (s // 2) * LANES : MAIN + (s // 2 + 1) * LANES]
+        tail = pltpu.roll(tail, TAIL, 1) if s % 2 else tail
+        parts = [jnp.where(lane < per, row[:, s * LANES : (s + 1) * LANES], 0.0), jnp.where(lane < per - LANES, tail, 0.0)]
+        total += pltpu.roll(jnp.concatenate(parts + [jnp.zeros((8, HEAD - 2 * LANES), F32)], axis=1), s * per, 1)
+    return total[0:1, 0:width].reshape(width)
+
+
+def finish_kernel(
+    features, towers, heads, sums,
+    out_features, out_class, out_bias_class, out_boxes, out_bias_boxes, out_head_class, out_head_class_bias,
+    out_head_boxes, out_head_boxes_bias,
+):
+    out_features[...] = features[...]
+    for i, (tower, bias, head, head_bias) in enumerate(
+        (
+            (out_class, out_bias_class, out_head_class, out_head_class_bias),
+            (out_boxes, out_bias_boxes, out_head_boxes, out_head_boxes_bias),
+        )
+    ):
+        tower[0] = towers[i]
+        bias[...] = sums[i, 0:LAYERS, 0:CH]
+        width = head.shape[0]
+        main, rest = min(width, LANES), max(0, width - LANES)
+        head[0:main, :] = heads[i, 0:ROWS, :].T[0:main, :]
+        if rest:
+            low = heads[i, ROWS:PACK, :]
+            both = jnp.concatenate([low, pltpu.roll(low, TAIL, 1)], axis=0)
+            head[LANES:width, :] = both.T[0:rest, :]
+        head_bias[...] = unlay(sums[i, LAYERS : LAYERS + 1, :], head_bias.shape[0])
 
 
 def fast(features, tower_class, bias_class, tower_boxes, bias_boxes, head_class, head_class_bias, head_boxes,
          head_boxes_bias, anchor_state, class_labels, box_targets, valid_rows):
     class_width, boxes_width = head_class_bias.shape[0], head_boxes_bias.shape[0]
-
-    def lay(vector):
-        parts = vector.reshape(SECTIONS, -1)
-        main = parts[:, :LANES]
-        rest = parts[:, LANES:]
-        main = jnp.pad(main, ((0, 0), (0, LANES - main.shape[1]))).reshape(-1)
-        rest = jnp.pad(rest, ((0, 0), (0, TAIL - rest.shape[1]))).reshape(-1)
-        return jnp.concatenate([main, rest])[None]
-
-    def unlay(row, width):
-        per = width // SECTIONS
-        main = row[: SECTIONS * LANES].reshape(SECTIONS, LANES)[:, : min(per, LANES)]
-        rest = row[SECTIONS * LANES :].reshape(SECTIONS, TAIL)[:, : max(0, per - LANES)]
-        return jnp.concatenate([main, rest], axis=1).reshape(width)
-
-    bias = jnp.stack(
-        [
-            jnp.concatenate([jnp.pad(tower, ((0, 0), (0, HEAD - CH))), lay(head), jnp.zeros((3, HEAD), F32)])
-            for tower, head in ((bias_class, head_class_bias), (bias_boxes, head_boxes_bias))
-        ]
-    )
+    spread, targets, mask_lab, mask_tgt, label = constants(class_width, boxes_width)
     tiles = features.shape[0]
     vmem = pl.BlockSpec(memory_space=pltpu.VMEM)
     smem = pl.BlockSpec(memory_space=pltpu.SMEM)
     v = lambda shape, dtype: pltpu.VMEM(shape, dtype)
     out = lambda shape, dtype: jax.ShapeDtypeStruct(shape, dtype)
-    results = pl.pallas_call(
+    anywhere = pl.BlockSpec(memory_space=pl.ANY)
+    raw = pl.pallas_call(
         head_kernel,
         out_shape=(
             out((tiles, 64, CH), BF16),
-            out((1, ROWS, CH), F32),
-            out((1, ROWS, CH), F32),
-            out(head_class.shape, F32),
-            out(head_boxes.shape, F32),
+            out((2, ROWS, CH), F32),
+            out((2, PACK, LANES), F32),
             out((2, 8, HEAD), F32),
         ),
-        in_specs=[vmem] * 9 + [smem] + [vmem] * 5,
-        out_specs=(vmem,) * 6,
+        in_specs=[vmem] * 12 + [smem, vmem] + [anywhere] * 4,
+        out_specs=(vmem,) * 4,
         scratch_shapes=[
+            v(spread.shape[1:], BF16),
+            v(targets.shape, BF16),
+            v(mask_lab.shape, BF16),
+            v(mask_tgt.shape, BF16),
+            v((8, HEAD), F32),
+            pltpu.SemaphoreType.DMA((4,)),
             v((2, ROWS, CH), BF16),
             v((2, PACK, LANES), BF16),
             v((LAYERS, DEEP, CH), BF16),
             v((DEEP, HEAD), BF16),
-            v((SECTIONS, PLANES, PACK, LANES), BF16),
+            v((SECTIONS, PLANES, HALF, LANES), BF16),
             v((LAYERS, DEEP, CH), BF16),
             v((DEEP, HEAD), BF16),
             v((LAYERS, PLANES, ROWS, CH), BF16),
             v((PLANES, ROWS, HEAD), BF16),
-            v((SECTIONS, PLANES, PACK, LANES), BF16),
-            v((LAYERS, PLANES, ROWS, CH), BF16),
-            v((SECTIONS, PLANES, PACK, LANES), BF16),
-            v((PLANES, ROWS, CH), BF16),
-            v((PLANES, PACK, LANES), BF16),
-            v((PLANES, ROWS, CH), BF16),
-            v((PLANES, PACK, LANES), BF16),
+            v((2, 2, PLANES, ROWS, LANES), BF16),
+            v((2, 2, PLANES, HALF, LANES), BF16),
+            v((LAYERS, 2, ROWS, LANES), BF16),
+            v((LAYERS, 2, HALF, CH), BF16),
+            v((PLANES, 2, ROWS, LANES), BF16),
+            v((PLANES, 2, HALF, LANES), BF16),
+            v((LAYERS, PLANES, HALF, LANES), BF16),
+            v((PLANES, ROWS, LANES), BF16),
+            v((PLANES, HALF, LANES), BF16),
+            v((LAYERS, PLANES, HALF, LANES), BF16),
+            v((PLANES, ROWS, LANES), BF16),
+            v((PLANES, HALF, LANES), BF16),
+            v((LAYERS, PLANES, HALF, LANES), BF16),
+            v((PLANES, ROWS, LANES), BF16),
+            v((PLANES, HALF, LANES), BF16),
+            v((LAYERS, 2, HALF, LANES), BF16),
+            v((SECTIONS, 2, HALF, LANES), BF16),
             v((2, PX + 2 * TILE, 3 * CH), BF16),
             v((2, PX + 2 * TILE, 3 * CH), BF16),
-            v((2, PX + 2 * TILE, 3 * HEAD), BF16),
-            v((LAYERS + 1, CH, 2 * PX), BF16),
+            v((2, PX + 2 * TILE, HEAD), BF16),
+            v((LAYERS, CH, 2 * PX), BF16),
+            v((3, CH, 2 * PX), BF16),
             v((LAYERS, 2 * PX, CH), F32),
             v((2 * PX, HEAD), F32),
             v((2 * PX, HEAD), F32),
-            v((2 * PX, HEAD), F32),
+            v((2 * PX, MAIN), F32),
             v((2 * PX, CH), F32),
             v((2, PX, CH), BF16),
             v((TILE, LAB + TGT), F32),
@@ -688,20 +824,31 @@
             collective_id=0, has_side_effects=True, vmem_limit_bytes=62 * 2**20
         ),
     )(
-        features.reshape(tiles, 64, CH), tower_class, tower_boxes, head_class, head_boxes, bias,
-        anchor_state, class_labels, box_targets, valid_rows, *constants(class_width, boxes_width),
-    )
-    grad_features, grad_class, grad_boxes, grad_head_class, grad_head_boxes, sums = results
+        features.reshape(tiles, 64, CH), tower_class, tower_boxes, head_class.T, head_boxes.T, bias_class, bias_boxes,
+        head_class_bias, head_boxes_bias, anchor_state, class_labels, box_targets, valid_rows, label,
+        spread, targets, mask_lab, mask_tgt,
+    )
+    results = pl.pallas_call(
+        finish_kernel,
+        out_shape=(
+            out((tiles, 64, CH), BF16),
+            out(tower_class.shape, F32),
+            out(bias_class.shape, F32),
+            out(tower_boxes.shape, F32),
+            out(bias_boxes.shape, F32),
+            out(head_class.shape[::-1], F32),
+            out(head_class_bias.shape, F32),
+            out(head_boxes.shape[::-1], F32),
+            out(head_boxes_bias.shape, F32),
+        ),
+        in_specs=[vmem] * 4,
+        out_specs=(vmem,) * 9,
+    )(*raw)
+    of_features, of_class, of_bias_class, of_boxes, of_bias_boxes, of_head_class, *rest = results
+    of_head_class_bias, of_head_boxes, of_head_boxes_bias = rest
     return (
-        grad_features.reshape(features.shape),
-        grad_class,
-        sums[0, :LAYERS, :CH],
-        grad_boxes,
-        sums[1, :LAYERS, :CH],
-        grad_head_class,
-        unlay(sums[0, LAYERS], class_width),
-        grad_head_boxes,
-        unlay(sums[1, LAYERS], boxes_width),
+        of_features.reshape(features.shape), of_class, of_bias_class, of_boxes, of_bias_boxes,
+        of_head_class.T, of_head_class_bias, of_head_boxes.T, of_head_boxes_bias,
     )
 
 

time: 154 us -> 104 us (0.68)
  Pallas kernels: 136 us -> 103 us
  local copies, waits for them, and re-layouts: 14.1 us -> 0 us
    pallas_call x1 -> x2, Pallas kernels: 136 us -> 103 us  [the longest x1 101 us: fast(): pl.pallas_call(head_kernel, out_shape=(out((tiles, 64, CH), BF16), out((2...]
    unnamed x15 -> x0, local copies, waits for them, and re-layouts: 8.31 us -> none
    reshape x8 -> x0, local copies, waits for them, and re-layouts: 2.94 us -> none  [the longest x2 1.5 us: lay(): parts = vector.reshape(SECTIONS, -1)]
where the time goes in v2:
time: 104 us
  Pallas kernels  103 us (99%)
    pallas_call x1, Pallas kernels, fast(): pl.pallas_call(head_kernel, out_shape=(out((tiles, 64, CH), BF16), out((2...  101 us
    pallas_call x1, Pallas kernels, fast(): pl.pallas_call(finish_kernel, out_shape=(out((tiles, 64, CH), BF16), out(...  2.44 us

profile of v2, /device:TPU:0, one launch (start us, length us, event | category | flops | bytes accessed | tf_op | source)
XLA Modules:
  0.0 104.0 jit_solution(16171524822942424436)
XLA Ops:
  0.6 100.9 %shard_map.241 = (bf16[4,64,256]{2,1,0:T(8,128)(2,1)}, f32[2,288,256]{2,1,0:T(8,128)}, f32[2,432,128]{2,1,0:T(8,128)}, f32[2,8,768]{2,1,0:T(8,128)}) custom-call(bf16[4,64,256]{2,1,0:T(8,128)(2,1)} %bitcast.7, f32[1,288,256]{2,1,0:T(8,128)} %tower_class.1, f32[1,288,256]{2,1,0:T(8,128)} %tower_boxes.1, f32[180,288]{1,0:T(8,128)} %bitcast.6, ...), custom_call_target="tpu_custom_call" | custom-call | tf_op jit(solution)/shard_map/pallas_call | solution.py:754
  101.6 2.4 %shard_map.242 = (bf16[4,64,256]{2,1,0:T(8,128)(2,1)}, f32[1,288,256]{2,1,0:T(8,128)}, f32[4,256]{1,0:T(4,128)}, f32[1,288,256]{2,1,0:T(8,128)}, f32[4,256]{1,0:...) custom-call(bf16[4,64,256]{2,1,0:T(8,128)(2,1)} %get-tuple-element.22.features, ...), custom_call_target="tpu_custom_call" | custom-call | tf_op jit(solution)/shard_map/pallas_call | solution.py:831

commit v3 on v2

--- a/solution.py
+++ b/solution.py
@@ -39,6 +39,9 @@
 LAB = 256
 TGT = 640
 DEEP = 9 * CH
+FOLD = 3
+FOLD_ROWS = ROWS // FOLD
+FOLD_LANES = 32
 
 
 def head_layout(width):
@@ -107,16 +110,33 @@
     return jnp.where(low, p, q_turned), jnp.where(low, p_turned, q)
 
 
+def folded(v):
+    parts = [v[i * FOLD_ROWS : (i + 1) * FOLD_ROWS] for i in range(FOLD)]
+    return parts[0] + sum(pltpu.roll(part, i * FOLD_LANES, 1) for i, part in enumerate(parts) if i)
+
+
+def unfolded(v):
+    v = v.astype(F32)
+    low = lax.broadcasted_iota(jnp.int32, v.shape, 1) < FOLD_LANES
+    return [
+        jnp.where(low, pltpu.roll(v, LANES - i * FOLD_LANES, 1) if i else v, 0.0) for i in range(FOLD)
+    ]
+
+
+def conv(act3, t, kernel, lanes=slice(None)):
+    return sum(
+        dot(act3[t, TILE * r : TILE * r + PX, :], kernel[3 * CH * r : 3 * CH * (r + 1), lanes]) for r in range(3)
+    )
+
+
 def forward_layer(m, l):
-    z = sum(dot(shifted_rows(m.act3, r), m.w[l, 3 * CH * r : 3 * CH * (r + 1), :]) for r in range(3))
-    z = z + m.bias[l : l + 1, 0:CH]
     for t in range(2):
-        zt = z[t * PX : (t + 1) * PX]
-        square = zt * zt
-        th = jnp.tanh(GELU_C * (zt + 0.044715 * zt * square))
+        z = conv(m.act3, t, m.w.at[l]) + m.bias[l : l + 1, 0:CH]
+        square = z * z
+        th = jnp.tanh(GELU_C * (z + 0.044715 * z * square))
         half = 0.5 * (1.0 + th)
-        a = zt * half
-        m.slope[l, t * PX : (t + 1) * PX, :] = half + (0.5 * GELU_C) * zt * (1.0 - th * th) * (
+        a = z * half
+        m.slope[l, t * PX : (t + 1) * PX, :] = half + (0.5 * GELU_C) * z * (1.0 - th * th) * (
             1.0 + (3 * 0.044715) * square
         )
         put_shifted(m.act3, t, a, 1, CH)
@@ -125,13 +145,6 @@
         else:
             for i, moved in enumerate((moved_right(a), a, moved_left(a))):
                 m.last_t[i, :, t * PX : (t + 1) * PX] = moved.T.astype(BF16)
-
-
-def head_forward(m, lanes):
-    for n in range(lanes.start, lanes.stop, 256):
-        m.logits[:, n : n + 256] = sum(
-            dot(shifted_rows(m.act3, r), m.wh[3 * CH * r : 3 * CH * (r + 1), n : n + 256]) for r in range(3)
-        )
 
 
 def expand(row, mask):
@@ -153,42 +166,39 @@
             )
 
 
-def loss_gradient(m, lanes):
+def head_gradients(m, lanes):
     total = m.count_sum[0:1, :] + m.count_in[1, 0:1, :] + m.count_in[2, 0:1, :] + m.count_in[3, 0:1, :]
-    width = lanes.stop - lanes.start
-    scale = jnp.concatenate([1.0 / jnp.maximum(total, 1.0)] * (width // LANES), axis=1)
-    bias = m.bias[4:5, lanes]
-
-    def keep(t, g):
-        g = g.astype(BF16)
-        m.grad_bias[4:5, lanes] += jnp.sum(g.astype(F32), axis=0, keepdims=True)
-        m.gl[t, TILE : TILE + PX, lanes] = g
-
-    @pl.when(m.role == 0)
-    def _():
-        for t in range(2):
-            at = slice(t * PX, (t + 1) * PX)
-            x = m.logits[at, lanes] + bias
-            code = m.code[at, lanes]
-            labeled = code == m.label[0:1, lanes]
-            y = jnp.where(labeled, -x, x)
-            e = jnp.exp(-jnp.abs(y))
-            more = 1.0 + e
-            q = jnp.where(y >= 0, 1.0, e) / more
-            softplus = jnp.maximum(y, 0.0) + jnp.log(more)
-            slope = q * q * (2.0 * (1.0 - q) * softplus + q)
-            keep(t, slope * (jnp.where(labeled, -0.25, jnp.where(code > 0.5, 0.75, 0.0)) * scale))
-
-    @pl.when(m.role == 1)
-    def _():
-        for t in range(2):
-            at = slice(t * PX, (t + 1) * PX)
-            if lanes.start < MAIN:
-                offset = m.logits[at, lanes] + bias - m.target[at, lanes]
-                g = jnp.where(m.code[at, lanes] > 1.5, jnp.clip(offset / huber_beta, -1.0, 1.0), 0.0)
-                keep(t, g * scale)
-            else:
-                m.gl[t, TILE : TILE + PX, lanes] = jnp.zeros((PX, width), BF16)
+    scale = jnp.concatenate([1.0 / jnp.maximum(total, 1.0)] * 2, axis=1)
+
+    def of_class(x, t, at):
+        code = m.code[t * PX : (t + 1) * PX, at]
+        labeled = code == m.label[0:1, at]
+        y = jnp.where(labeled, -x, x)
+        e = jnp.exp(-jnp.abs(y))
+        more = 1.0 + e
+        q = jnp.where(y >= 0, 1.0, e) / more
+        softplus = jnp.maximum(y, 0.0) + jnp.log(more)
+        slope = q * q * (2.0 * (1.0 - q) * softplus + q)
+        return slope * (jnp.where(labeled, -0.25, jnp.where(code > 0.5, 0.75, 0.0)) * scale)
+
+    def of_boxes(x, t, at):
+        rows = slice(t * PX, (t + 1) * PX)
+        g = jnp.clip((x - m.target[rows, at]) / huber_beta, -1.0, 1.0)
+        return jnp.where(m.code[rows, at] > 1.5, g, 0.0) * scale
+
+    def run(gradient):
+        blocks = [(t, slice(n, n + 256)) for n in range(lanes.start, lanes.stop, 256) for t in range(2)]
+        logits = [conv(m.act3, blocks[0][0], m.wh, blocks[0][1])]
+        for i, (t, at) in enumerate(blocks):
+            if i + 1 < len(blocks):
+                logits.append(conv(m.act3, blocks[i + 1][0], m.wh, blocks[i + 1][1]))
+            g = gradient(logits[i] + m.bias[4:5, at], t, at).astype(BF16)
+            m.grad_bias[4:5, at] += jnp.sum(g.astype(F32), axis=0, keepdims=True)
+            m.gl[t, TILE : TILE + PX, at] = g
+
+    pl.when(m.role == 0)(lambda: run(of_class))
+    if lanes.start < MAIN:
+        pl.when(m.role == 1)(lambda: run(of_boxes))
 
 
 def head_kernel_gradient(m, lanes, r):
@@ -197,39 +207,39 @@
         m.gh[at : at + CH, lanes] = dot(m.last_t[s], shifted_rows(m.gl, 2 - r, lanes)).astype(BF16)
 
 
-def head_input_gradient(m):
-    columns = []
-    for s in range(3):
-        acc = None
-        for r in range(3):
-            at = (3 * r + s) * CH
-            part = dot_nt(shifted_rows(m.gl, 2 - r), m.wh[at : at + CH, :])
-            acc = part if acc is None else acc + part
-        columns.append(acc)
+def head_input_gradient(m, lanes):
     for t in range(2):
-        at = slice(t * PX, (t + 1) * PX)
-        m.da[at, :] = moved_left(columns[0][at]) + columns[1][at] + moved_right(columns[2][at])
-
-
-def input_gradient(m, g3, kernel):
+        columns = []
+        for s in range(3):
+            acc = None
+            for r in range(3):
+                at = (3 * r + s) * CH
+                g = m.gl[t, TILE * (2 - r) : TILE * (2 - r) + PX, lanes]
+                part = dot_nt(g, m.wh[at : at + CH, lanes])
+                acc = part if acc is None else acc + part
+            columns.append(acc)
+        layer_upstream(m, LAYERS - 1, t, moved_left(columns[0]) + columns[1] + moved_right(columns[2]))
+
+
+def input_gradient(m, l, t):
     acc = None
     for r in range(3):
         for s in range(3):
             at = (3 * r + s) * CH
-            part = dot_nt(shifted_rows(g3, 2 - r, slice(s * CH, (s + 1) * CH)), kernel[at : at + CH, :])
+            g = m.g3[l, t, TILE * (2 - r) : TILE * (2 - r) + PX, s * CH : (s + 1) * CH]
+            part = dot_nt(g, m.w[l, at : at + CH, :])
             acc = part if acc is None else acc + part
     return acc
 
 
-def layer_upstream(m, l):
-    g = (m.da[...] * m.slope[l]).astype(BF16).astype(F32)
-    m.grad_bias[l : l + 1, 0:CH] = jnp.sum(g, axis=0, keepdims=True)
-    for t in range(2):
-        put_shifted(m.g3, t, g[t * PX : (t + 1) * PX], -1, CH)
+def layer_upstream(m, l, t, da):
+    g = (da * m.slope[l, t * PX : (t + 1) * PX, :]).astype(BF16).astype(F32)
+    m.grad_bias[l : l + 1, 0:CH] += jnp.sum(g, axis=0, keepdims=True)
+    put_shifted(m.g3.at[l], t, g, -1, CH)
 
 
 def layer_kernel_gradient(m, l, r):
-    part = dot(m.act_t[l], shifted_rows(m.g3, 2 - r))
+    part = dot(m.act_t[l], shifted_rows(m.g3.at[l], 2 - r))
     for s in range(3):
         at = (3 * r + s) * CH
         m.g[l, at : at + CH, :] = part[:, s * CH : (s + 1) * CH].astype(BF16)
@@ -257,8 +267,12 @@
             pl.when(when)(copy.start)
         self.sent.append((when, copy))
 
-    def arrived(self, name, dst, peer, **at):
-        self.copy(name, dst, dst, peer, **at).wait_recv()
+    def arrived(self, name, dst, peer, when=None, **at):
+        copy = self.copy(name, dst, dst, peer, **at)
+        if when is None:
+            copy.wait_recv()
+        else:
+            pl.when(when)(copy.wait_recv)
 
     def finish(self):
         for when, copy in self.sent:
@@ -268,18 +282,19 @@
                 pl.when(when)(copy.wait_send)
 
 
-SEMAPHORES = 192
+SEMAPHORES = 224
 WAYS = {
     "T0": "A", "T1": "B", "T3": "A", "T2": "B", "M0": "B", "M1": "A", "M3": "B", "M2": "A", "U0": "A", "U1": "B", "U3": "A", "U2": "B",
 }
 SCHEDULE = (
-    "aT0", "zT", "f", "aM0", "aT1", "bM0", "bT0", "zM", "e", "bT1", "aT3", "aT2", "cT1", "zU", "cM0", "bT3", "bT2",
-    "aM2", "aM1", "aU0", "cT0", "aM3", "y", "aU1", "cT3", "cT2", "F0", "bM2", "F1", "bM3", "bM1", "aU2", "F2",
-    "cM2", "bU0", "aU3", "F3", "cM1", "cM3", "bU2", "bU1", "cU0", "bU3", "HM", "cU3", "WM0", "WM1", "WM2", "cU2",
-    "kM0", "cU1", "kM2", "kM3", "kM1", "HU", "X", "u3", "pM0", "pM3", "w3", "x3", "k3", "u2", "pM2", "w2", "pM1",
-    "x2", "k2", "qM0", "u1", "x1", "w1", "qM2", "qM1", "p3", "u0", "WU0", "qM3", "WU1", "k1", "WU2", "w0", "p2",
-    "k0", "q3", "p1", "x0", "kU2", "q2", "s3", "p0", "kU3", "Bk", "q1", "kU1", "kU0", "q0", "Bp", "D", "pU3", "s2",
-    "pU0", "sM", "pU1", "Bq", "s1", "E", "pU2", "qU0", "s0", "qU3", "qU1", "qU2", "Bs", "t", "sU",
+    "zT", "aM0", "aT0", "aU0", "aT1", "bT0", "f", "aT3", "bT1", "bM0", "zU", "aT2", "zM", "bU0", "e", "aU1", "aU3",
+    "bT3", "bT2", "bU3", "aM1", "bU1", "aU2", "aM2", "cU0", "cT0", "y", "cT3", "cM0", "cT1", "cU3", "aM3", "cU1",
+    "cT2", "bM1", "bU2", "F0", "bM2", "cU2", "bM3", "F1", "F2", "cM1", "dU3", "cM3", "cM2", "F3", "HM", "dU2",
+    "dU0", "dU1", "WM0", "WM1", "HU", "X", "kM1", "kM0", "WU0", "w3", "x3", "kU0", "WU1", "k3", "w2", "kU1", "WU2",
+    "x2", "k2", "kU2", "w1", "x1", "p3", "kU3", "Bk", "p2", "k1", "w0", "WM2", "Bp", "q2", "k0", "x0", "p1", "rU0",
+    "q3", "kM3", "kM2", "Bq", "rU1", "rU2", "rU3", "q1", "pU0", "p0", "pM2", "pM0", "pM3", "s2", "q0", "pU3", "Bs",
+    "pU1", "s3", "qU0", "pU2", "s1", "pM1", "D", "qM3", "qM0", "qM2", "s0", "qM1", "E", "qU3", "qU1", "qU2", "sM",
+    "t", "sU",
 )
 
 
@@ -288,8 +303,9 @@
     state, labels, targets_in, valid, label, spread_any, targets_any, mask_lab_any, mask_tgt_any,
     out_features, out_towers, out_heads, out_bias,
     spread, targets, mask_lab, mask_tgt, bias, fetch_sem,
-    own, own_h, w, wh, hp, g, gh, rc, rch, sm, su, r1a, r1b, r1m, r1u, r2, r2m, r2u, quarter, sum_m, sum_u, rz, rzm, rzu, done, layer_in,
-    act3, g3, gl, act_t, last_t, slope, logits, code, target, da,
+    own, own_h, own_v, w, wh, hp, hv, g, gh, rc, rch, sm, su, sv, r1a, r1b, r1m, r1u, r1v, r2, r2m, r2u, r2v,
+    quarter, sum_m, sum_u, sum_v, rz, rzm, rzu, rzv, done, layer_in,
+    act3, g3, gl, act_t, last_t, slope, spare, code, target, da,
     x, lab, lab_in, count_mine, count_sum, count_in, grad_bias, bias_in, bias_z, dx, dx_in, tile_out, features_in,
     send_sem, recv_sem,
 ):
@@ -301,10 +317,11 @@
     to_z = lambda k: (s, 2 * plane(k) + my_c)
     to_pair = (s, 2 * (my_z + 1 - 2 * (my_z % 2)) + my_c)
     role = my_z % 2
+    on_class, on_boxes = role == 0, role == 1
     net = Traffic(send_sem, recv_sem)
     m = SimpleNamespace(
-        w=w, wh=wh, g=g, gh=gh, act3=act3, g3=g3, gl=gl, act_t=act_t, last_t=last_t, slope=slope, logits=logits, code=code,
-        target=target, da=da, lab=lab, lab_in=lab_in, count_sum=count_sum, count_in=count_in, grad_bias=grad_bias,
+        w=w, wh=wh, g=g, gh=gh, act3=act3, g3=g3, gl=gl, act_t=act_t, last_t=last_t, slope=slope, code=code,
+        target=target, lab=lab, lab_in=lab_in, count_sum=count_sum, count_in=count_in, grad_bias=grad_bias,
         bias=bias, spread=spread, targets=targets, mask_lab=mask_lab, mask_tgt=mask_tgt, label=label, role=role,
     )
 
@@ -325,18 +342,15 @@
     for copy in constants_in:
         copy.start()
 
-    for role_at, (tower, head) in enumerate(((tower_class, head_class), (tower_boxes, head_boxes))):
-        own[role_at] = tower[0].astype(BF16)
-        width = head.shape[0]
-        main = min(width, LANES)
-        own_h[role_at] = jnp.zeros((PACK, LANES), BF16)
-        own_h[role_at, 0:ROWS, 0:main] = head[0:main, :].T.astype(BF16)
-        if width > LANES:
-            logits[0:ROWS, 0:LANES] = jnp.zeros((ROWS, LANES), F32)
-            logits[0:ROWS, 0 : width - LANES] = head[LANES:width, :].T
-            own_h[role_at, ROWS:PACK, :] = (
-                logits[0:HALF, 0:LANES] + pltpu.roll(logits[HALF:ROWS, 0:LANES], TAIL, 1)
-            ).astype(BF16)
+    own[0] = tower_class[0].astype(BF16)
+    own[1] = tower_boxes[0].astype(BF16)
+    own_h[0:ROWS, :] = head_class[0:LANES, :].T.astype(BF16)
+    rest, narrow = head_class.shape[0] - LANES, head_boxes.shape[0]
+    spare[...] = jnp.zeros((ROWS, 2 * LANES), F32)
+    spare[:, 0:rest] = head_class[LANES : LANES + rest, :].T
+    spare[:, LANES : LANES + narrow] = head_boxes[...].T
+    own_h[ROWS:PACK, :] = (spare[0:HALF, 0:LANES] + pltpu.roll(spare[HALF:ROWS, 0:LANES], TAIL, 1)).astype(BF16)
+    own_v[...] = folded(spare[:, LANES : 2 * LANES]).astype(BF16)
 
     row = lax.broadcasted_iota(jnp.int32, (TILE, TILE * A), 0)
     found = jnp.zeros((TILE, TILE * A), F32)
@@ -355,6 +369,12 @@
 
     pl.semaphore_wait(barrier, len(peers))
 
+    def kinds(kind_name):
+        return ("M", "V") if kind_name == "M" else (kind_name,)
+
+    def due(kind_name):
+        return dict(T=None, M=on_class, U=on_boxes, V=on_boxes)[kind_name]
+
     def head_lanes(sec):
         return pl.ds(pl.multiple_of(LANES * sec, LANES), LANES)
 
@@ -363,18 +383,23 @@
             return w.at[sec, shard(z, my_c), :]
         if kind_name == "M":
             return wh.at[shard(z, my_c), head_lanes(sec)]
+        if kind_name == "V":
+            return hv.at[sec, z]
         return hp.at[sec, z]
 
     def own_shard(kind_name, which):
         if kind_name == "T":
             return own.at[which]
-        return own_h.at[which, pl.ds(0, ROWS) if kind_name == "M" else pl.ds(ROWS, HALF), :]
+        if kind_name == "V":
+            return own_v
+        return own_h.at[pl.ds(0, ROWS) if kind_name == "M" else pl.ds(ROWS, HALF), :]
 
     def planes_send(kind_name):
         for k in (1, 3, 2):
-            net.send(
-                ("z", kind_name, k), own_shard(kind_name, plane(k) % 2), place(kind_name, s, my_z), to_z(k)
-            )
+            other = plane(k) % 2
+            for kind in kinds(kind_name):
+                when = dict(T=None, M=other == 0, U=other == 1, V=other == 1)[kind]
+                net.send(("z", kind, k), own_shard(kind, other), place(kind, s, my_z), to_z(k), when)
 
     in_plane = (("x", to_x, sx), ("y", to_y, sy), ("g", to_g, sg))
 
@@ -391,53 +416,78 @@
         return place(kind_name, sec, (my_z + PLANES - j) % PLANES)
 
     def ways(kind_name, j):
-        if WAYS[kind_name + str(j)] == "A":
+        if WAYS[kind_name.replace("V", "M") + str(j)] == "A":
             return (to_x, sx), (to_y, sy)
         return (to_y, sy), (to_x, sx)
 
     def gather_mine(kind_name, j):
-        mine = piece(kind_name, s, j)
-        if j:
-            net.arrived(("z", kind_name, j), mine, to_z(PLANES - j))
-        for (n, _), name in zip(ways(kind_name, j), ("g1", "g2")):
-            net.send((name, kind_name, j), mine, mine, n)
+        for kind in kinds(kind_name):
+            mine = piece(kind, s, j)
+            if j:
+                net.arrived(("z", kind, j), mine, to_z(PLANES - j), due(kind))
+            for (n, _), name in zip(ways(kind, j), ("g1", "g2")):
+                net.send((name, kind, j), mine, mine, n, due(kind))
         if kind_name == "T":
-            net.send(("swap", kind_name, j, 0), mine, mine, to_c)
+            net.send(("swap", "T", j, 0), mine, mine, to_c)
 
     def gather_pass(kind_name, j):
         (n1, s1), (n2, s2) = ways(kind_name, j)
-        first = piece(kind_name, s1, j)
-        net.arrived(("g1", kind_name, j), first, n1)
-        net.send(("g3", kind_name, j), first, first, n2)
+        for kind in kinds(kind_name):
+            first = piece(kind, s1, j)
+            net.arrived(("g1", kind, j), first, n1, due(kind))
+            net.send(("g3", kind, j), first, first, n2, due(kind))
         if kind_name == "T":
-            net.send(("swap", kind_name, j, 1), first, first, to_c)
+            net.send(("swap", "T", j, 1), first, first, to_c)
 
     def gather_last(kind_name, j):
         (n1, s1), (n2, s2) = ways(kind_name, j)
         for i, (name, sec) in enumerate((("g2", s2), ("g3", sg))):
-            got = piece(kind_name, sec, j)
-            net.arrived((name, kind_name, j), got, n2)
+            for kind in kinds(kind_name):
+                got = piece(kind, sec, j)
+                net.arrived((name, kind, j), got, n2, due(kind))
             if kind_name == "T":
-                net.send(("swap", kind_name, j, 2 + i), got, got, to_c)
+                net.send(("swap", "T", j, 2 + i), got, got, to_c)
         z = (my_z + PLANES - j) % PLANES
         at = pl.multiple_of(ROWS * (2 * z + my_c), 16)
         if kind_name == "M":
+
+            @pl.when(on_boxes)
+            def _():
+                for sec in range(SECTIONS):
+                    for i, part in enumerate(unfolded(hv[sec, z])):
+                        rows = pl.ds(at + i * FOLD_ROWS, FOLD_ROWS)
+                        wh[rows, sec * LANES : (sec + 1) * LANES] = part.astype(BF16)
+
             block = wh.at[pl.ds(at, ROWS), 0:MAIN]
             net.send(("swap", "M", j), block, block, to_c)
         if kind_name == "U":
-            for q in range(2):
-                lanes = slice((SECTIONS + q) * LANES, (SECTIONS + q + 1) * LANES)
-                top, bottom = swap_halves(hp[2 * q, z], hp[2 * q + 1, z])
-                wh[pl.ds(at, HALF), lanes] = top.astype(BF16)
-                wh[pl.ds(at + HALF, HALF), lanes] = bottom.astype(BF16)
+
+            @pl.when(on_boxes)
+            def _():
+                for q in range(2):
+                    lanes = slice((SECTIONS + q) * LANES, (SECTIONS + q + 1) * LANES)
+                    top, bottom = swap_halves(hp[2 * q, z], hp[2 * q + 1, z])
+                    wh[pl.ds(at, HALF), lanes] = top.astype(BF16)
+                    wh[pl.ds(at + HALF, HALF), lanes] = bottom.astype(BF16)
+
             block = wh.at[pl.ds(at, ROWS), MAIN:HEAD]
-            net.send(("swap", "U", j), block, block, to_c)
+            net.send(("up", j), block, block, to_pair, on_boxes)
+
+    def relayed_plane(j):
+        return (my_z + 1 + PLANES - j) % PLANES
+
+    def gather_relayed(kind_name, j):
+        block = wh.at[shard(relayed_plane(j), my_c), MAIN:HEAD]
+        net.arrived(("up", j), block, to_pair, on_class)
+        net.send(("swap", "U", j), block, block, to_c, on_class)
 
     def swapped(kind_name, j):
         z = (my_z + PLANES - j) % PLANES
-        if kind_name != "T":
-            lanes = slice(0, MAIN) if kind_name == "M" else slice(MAIN, HEAD)
-            net.arrived(("swap", kind_name, j), wh.at[shard(z, 1 - my_c), lanes], to_c)
+        if kind_name == "M":
+            net.arrived(("swap", "M", j), wh.at[shard(z, 1 - my_c), 0:MAIN], to_c)
+            return
+        if kind_name == "U":
+            net.arrived(("swap", "U", j), wh.at[shard(relayed_plane(j), 1 - my_c), MAIN:HEAD], to_c, on_class)
             return
         (_, s1), (_, s2) = ways(kind_name, j)
         for i, sec in enumerate((s, s1, s2, sg)):
@@ -454,7 +504,7 @@
             net.send(("count", k), count_sum, count_in.at[k], to_z(k))
 
     def prepare():
-        for ref in (act3, g3, gl):
+        for ref in (act3, *(g3.at[l] for l in range(LAYERS)), gl):
             for t in range(2):
                 ref[t, 0:TILE, :] = jnp.zeros((TILE, ref.shape[2]), BF16)
                 ref[t, TILE + PX : 2 * TILE + PX, :] = jnp.zeros((TILE, ref.shape[2]), BF16)
@@ -483,16 +533,20 @@
                 net.arrived(("count", k), count_in.at[k], to_z(PLANES - k))
         for j in range(PLANES):
             swapped(kind_name, j)
-        head_forward(m, head_part[kind_name])
-        loss_gradient(m, head_part[kind_name])
+        head_gradients(m, head_part[kind_name])
 
     head_part = dict(M=slice(0, MAIN), U=slice(MAIN, HEAD))
     w[s, shard(my_z, my_c), :] = own[role]
-    wh[shard(my_z, my_c), head_lanes(s)] = own_h[role, 0:ROWS, :]
-    hp[s, my_z] = own_h[role, ROWS:PACK, :]
-
-    def added(*values):
-        return sum(v.astype(F32) for v in values).astype(BF16)
+    hp[s, my_z] = own_h[ROWS:PACK, :]
+    hv[s, my_z] = own_v[...]
+
+    @pl.when(on_class)
+    def _():
+        wh[shard(my_z, my_c), head_lanes(s)] = own_h[0:ROWS, :]
+
+
+    def added(a, b):
+        return a + b
 
     def half_rows(which):
         return pl.ds(pl.multiple_of(HALF * which, 16), HALF)
@@ -503,7 +557,8 @@
     def core_send(l, zp):
         theirs = shard(zp, 1 - my_c)
         if l in head_part:
-            net.send(("rc", l, zp), gh.at[theirs, head_part[l]], rch.at[zp, :, head_part[l]], to_c)
+            when = on_class if l == "U" else None
+            net.send(("rc", l, zp), gh.at[theirs, head_part[l]], rch.at[zp, :, head_part[l]], to_c, when)
         else:
             net.send(("rc", l, zp), g.at[l, theirs, :], rc.at[l, zp], to_c)
 
@@ -563,57 +618,114 @@
             for i in range(2):
                 out_towers[i, half_rows(sec // 2), half_lanes(sec % 2)] = layer_in[sec, i].astype(F32)
 
-    def head_refs(kind_name):
-        return (sm, r1m, r2m, sum_m, rzm) if kind_name == "M" else (su, r1u, r2u, sum_u, rzu)
+    def head_refs(kind):
+        return dict(
+            M=(sm, r1m, r2m, sum_m, rzm), U=(su, r1u, r2u, sum_u, rzu), V=(sv, r1v, r2v, sum_v, rzv)
+        )[kind]
+
+    def both_cores(zp, rows, lanes):
+        at = pl.multiple_of(ROWS * (2 * zp + my_c) + rows[0], 16)
+        mine = gh[pl.ds(at, rows[1]), lanes]
+        return rch[zp, rows[0] : rows[0] + rows[1], lanes].astype(F32) + mine.astype(F32)
 
     def head_cores(kind_name, zp):
-        lanes = head_part[kind_name]
-        net.arrived(("rc", kind_name, zp), rch.at[zp, :, lanes], to_c)
-        at = pl.multiple_of(ROWS * (2 * zp + my_c), 16)
-        into, landing = head_refs(kind_name)[:2]
+        landed = rch.at[zp, :, head_part[kind_name]]
         if kind_name == "M":
-            for sec in range(SECTIONS):
-                lanes = slice(sec * LANES, (sec + 1) * LANES)
-                into[sec // 2, sec % 2, zp] = added(rch[zp, :, lanes], gh[pl.ds(at, ROWS), lanes])
-        else:
+            net.arrived(("rc", "M", zp), landed, to_c)
+
+            def store(kind):
+                for sec in range(SECTIONS):
+                    v = both_cores(zp, (0, ROWS), slice(sec * LANES, (sec + 1) * LANES))
+                    v = v if kind == "M" else folded(v)
+                    head_refs(kind)[0][sec // 2, sec % 2, zp] = v.astype(BF16)
+
+            for kind in kinds("M"):
+                pl.when(due(kind))(functools.partial(store, kind))
+            head_first_send("M", zp)
+            return
+        net.arrived(("rc", "U", zp), landed, to_c, on_class)
+
+        @pl.when(on_class)
+        def _():
             for q in range(2):
                 lanes = slice((SECTIONS + q) * LANES, (SECTIONS + q + 1) * LANES)
-                top = rch[zp, 0:HALF, lanes].astype(F32) + gh[pl.ds(at, HALF), lanes].astype(F32)
-                bottom = rch[zp, HALF:ROWS, lanes].astype(F32) + gh[pl.ds(at + HALF, HALF), lanes].astype(F32)
-                left, right = swap_halves(top, bottom)
-                into[q, 0, zp] = left.astype(BF16)
-                into[q, 1, zp] = right.astype(BF16)
-        if zp % 2 == 0:
-            net.send(("h1", kind_name, zp), into.at[:, 1 - my_x, zp], landing.at[zp], to_x)
-        else:
-            net.send(("h1", kind_name, zp), into.at[1 - my_y, :, zp], landing.at[zp], to_y)
+                left, right = swap_halves(both_cores(zp, (0, HALF), lanes), both_cores(zp, (HALF, HALF), lanes))
+                su[q, 0, zp] = left.astype(BF16)
+                su[q, 1, zp] = right.astype(BF16)
+
+        block = su.at[:, :, zp]
+        net.send(("ru", zp), block, block, to_pair, on_class)
+
+    def head_relayed(kind_name, zp):
+        net.arrived(("ru", zp), su.at[:, :, zp], to_pair, on_boxes)
+        head_first_send(kind_name, zp)
+
+    def head_first_send(kind_name, zp):
+        for kind in kinds(kind_name):
+            into, landing = head_refs(kind)[:2]
+            if zp % 2 == 0:
+                net.send(("h1", kind, zp), into.at[:, 1 - my_x, zp], landing.at[zp], to_x, due(kind))
+            else:
+                net.send(("h1", kind, zp), into.at[1 - my_y, :, zp], landing.at[zp], to_y, due(kind))
 
     def head_plane(kind_name, zp):
-        into, landing, landing2 = head_refs(kind_name)[:3]
-        net.arrived(("h1", kind_name, zp), landing.at[zp], to_x if zp % 2 == 0 else to_y)
-        for i in range(2):
-            at = (i, my_x, zp) if zp % 2 == 0 else (my_y, i, zp)
-            into[at] = added(into[at], landing[zp, i])
-        if zp % 2 == 0:
-            net.send(("h2", kind_name, zp), into.at[1 - my_y, my_x, zp], landing2.at[zp], to_y)
-        else:
-            net.send(("h2", kind_name, zp), into.at[my_y, 1 - my_x, zp], landing2.at[zp], to_x)
+        for kind in kinds(kind_name):
+            into, landing, landing2 = head_refs(kind)[:3]
+            net.arrived(("h1", kind, zp), landing.at[zp], to_x if zp % 2 == 0 else to_y, due(kind))
+
+            @pl.when(due(kind))
+            def _():
+                for i in range(2):
+                    at = (i, my_x, zp) if zp % 2 == 0 else (my_y, i, zp)
+                    into[at] = added(into[at], landing[zp, i])
+
+            if zp % 2 == 0:
+                net.send(("h2", kind, zp), into.at[1 - my_y, my_x, zp], landing2.at[zp], to_y, due(kind))
+            else:
+                net.send(("h2", kind, zp), into.at[my_y, 1 - my_x, zp], landing2.at[zp], to_x, due(kind))
 
     def head_planes(kind_name, zp):
-        into, _, landing2, total, others = head_refs(kind_name)
-        net.arrived(("h2", kind_name, zp), landing2.at[zp], to_y if zp % 2 == 0 else to_x)
-        total[zp] = added(into[my_y, my_x, zp], landing2[zp])
         k = (zp + PLANES - my_z) % PLANES
-        net.send(
-            ("hz", kind_name), total.at[zp], others.at[my_z], (s, 2 * zp + my_c), my_z != zp, span=PLANES, offset=k
-        )
+        for kind in kinds(kind_name):
+            into, _, landing2, total, others = head_refs(kind)
+            net.arrived(("h2", kind, zp), landing2.at[zp], to_y if zp % 2 == 0 else to_x, due(kind))
+
+            @pl.when(due(kind))
+            def _():
+                total[zp] = added(into[my_y, my_x, zp], landing2[zp])
+
+            away = jnp.logical_and(due(kind), my_z != zp)
+            to_zp = (s, 2 * zp + my_c)
+            net.send(("hz", kind), total.at[zp], others.at[my_z], to_zp, away, span=PLANES, offset=k)
 
     def head_store(kind_name):
-        total, others = head_refs(kind_name)[3:]
-        same, other = from_planes(("hz", kind_name), total, others)
-        at = slice(0, ROWS) if kind_name == "M" else slice(ROWS, PACK)
-        out_heads[role, at] = same
-        out_heads[1 - role, at] = other
+        for kind in kinds(kind_name):
+            total, others = head_refs(kind)[3:]
+            here = due(kind)
+            for k in (1, 2, 3):
+                when = here if k == 2 else jnp.logical_not(here)
+                source = others.at[plane(PLANES - k)]
+                net.arrived(("hz", kind), source, to_z(PLANES - k), when, span=PLANES, offset=k)
+
+            def store(v):
+                if kind == "M":
+                    out_heads[0, 0:ROWS] = v
+                elif kind == "U":
+                    out_heads[0, ROWS:PACK] = v
+                else:
+                    for i, part in enumerate(unfolded(v)):
+                        out_heads[1, i * FOLD_ROWS : (i + 1) * FOLD_ROWS] = part
+
+            @pl.when(here)
+            def _():
+                store(total[my_z].astype(F32) + others[plane(2)].astype(F32))
+
+            @pl.when(jnp.logical_not(here))
+            def _():
+                store(others[plane(1)].astype(F32) + others[plane(3)].astype(F32))
+
+        if kind_name == "U":
+            out_heads[1, ROWS:PACK] = jnp.zeros((HALF, LANES), F32)
 
     def bias_cores():
         net.arrived("bias c", bias_in.at[0], to_c)
@@ -639,7 +751,7 @@
 
     def features_sum():
         net.arrived("dx", dx_in, to_pair)
-        tile_out[...] = (da[0:PX, :] + dx_in[...].astype(F32)).astype(BF16)
+        tile_out[...] = (da[...] + dx_in[...].astype(F32)).astype(BF16)
         for name, peer, sec in in_plane:
             net.send(("b", name), tile_out.at[rows_of(sec), :], features_in.at[s], peer)
 
@@ -650,36 +762,43 @@
         out_features[s] = tile_out[rows_of(s), :]
 
     def head_gradient(kind_name, r):
-        head_kernel_gradient(m, head_part[kind_name], r)
+        if kind_name == "M":
+            head_kernel_gradient(m, head_part["M"], r)
+        else:
+            pl.when(on_class)(lambda: head_kernel_gradient(m, head_part["U"], r))
         for zp in ((0,), (1,), (2, 3))[r]:
             core_send(kind_name, zp)
 
     def head_input():
-        head_input_gradient(m)
-
-    def upstream(l):
-        layer_upstream(m, l)
-        if l == 0:
-            net.send("bias c", grad_bias, bias_in.at[0], to_c)
+        pl.when(on_class)(lambda: head_input_gradient(m, slice(0, HEAD)))
+        pl.when(on_boxes)(lambda: head_input_gradient(m, slice(0, MAIN)))
 
     def layer_gradient(l):
         for r in range(3):
             layer_kernel_gradient(m, l, r)
-            for zp in ((0,), (1,), (2, 3))[r]:
-                core_send(l, zp)
+        for zp in range(PLANES):
+            core_send(l, zp)
 
     def layer_input(l):
-        da[...] = input_gradient(m, g3, w.at[l])
+        for t in range(2):
+            v = input_gradient(m, l, t)
+            if l:
+                layer_upstream(m, l - 1, t, v)
+            elif t == 0:
+                da[...] = v
+            else:
+                dx[...] = v.astype(BF16)
         if l == 0:
-            dx[...] = da[PX : 2 * PX, :].astype(BF16)
             net.send("dx", dx, dx_in, to_pair)
+        if l == 1:
+            net.send("bias c", grad_bias, bias_in.at[0], to_c)
 
     def either(of_head, of_tower):
         return lambda *which: of_head(*which) if which[0] in head_part else of_tower(*which)
 
     steps = dict(
-        z=planes_send, f=features_send, e=features_tile, y=prepare, a=gather_mine, b=gather_pass, c=gather_last,
-        F=forward, H=head, W=head_gradient, X=head_input, u=upstream, w=layer_gradient, x=layer_input,
+        d=gather_relayed, r=head_relayed, z=planes_send, f=features_send, e=features_tile, y=prepare, a=gather_mine, b=gather_pass, c=gather_last,
+        F=forward, H=head, W=head_gradient, X=head_input, w=layer_gradient, x=layer_input,
         k=either(head_cores, tower_cores), p=either(head_plane, tower_plane), q=either(head_planes, tower_planes),
         s=either(head_store, tower_sum), t=tower_store, D=features_sum, E=features_store,
         B=lambda which: dict(k=bias_cores, p=bias_plane, q=bias_planes, s=bias_store)[which](),
@@ -769,41 +888,48 @@
             v((8, HEAD), F32),
             pltpu.SemaphoreType.DMA((4,)),
             v((2, ROWS, CH), BF16),
-            v((2, PACK, LANES), BF16),
+            v((PACK, LANES), BF16),
+            v((FOLD_ROWS, LANES), BF16),
             v((LAYERS, DEEP, CH), BF16),
             v((DEEP, HEAD), BF16),
             v((SECTIONS, PLANES, HALF, LANES), BF16),
+            v((SECTIONS, PLANES, FOLD_ROWS, LANES), BF16),
             v((LAYERS, DEEP, CH), BF16),
             v((DEEP, HEAD), BF16),
             v((LAYERS, PLANES, ROWS, CH), BF16),
             v((PLANES, ROWS, HEAD), BF16),
             v((2, 2, PLANES, ROWS, LANES), BF16),
             v((2, 2, PLANES, HALF, LANES), BF16),
+            v((2, 2, PLANES, FOLD_ROWS, LANES), BF16),
             v((LAYERS, 2, ROWS, LANES), BF16),
             v((LAYERS, 2, HALF, CH), BF16),
             v((PLANES, 2, ROWS, LANES), BF16),
             v((PLANES, 2, HALF, LANES), BF16),
+            v((PLANES, 2, FOLD_ROWS, LANES), BF16),
             v((LAYERS, PLANES, HALF, LANES), BF16),
             v((PLANES, ROWS, LANES), BF16),
             v((PLANES, HALF, LANES), BF16),
+            v((PLANES, FOLD_ROWS, LANES), BF16),
             v((LAYERS, PLANES, HALF, LANES), BF16),
             v((PLANES, ROWS, LANES), BF16),
             v((PLANES, HALF, LANES), BF16),
+            v((PLANES, FOLD_ROWS, LANES), BF16),
             v((LAYERS, PLANES, HALF, LANES), BF16),
             v((PLANES, ROWS, LANES), BF16),
             v((PLANES, HALF, LANES), BF16),
+            v((PLANES, FOLD_ROWS, LANES), BF16),
             v((LAYERS, 2, HALF, LANES), BF16),
             v((SECTIONS, 2, HALF, LANES), BF16),
             v((2, PX + 2 * TILE, 3 * CH), BF16),
-            v((2, PX + 2 * TILE, 3 * CH), BF16),
+            v((LAYERS, 2, PX + 2 * TILE, 3 * CH), BF16),
             v((2, PX + 2 * TILE, HEAD), BF16),
             v((LAYERS, CH, 2 * PX), BF16),
             v((3, CH, 2 * PX), BF16),
             v((LAYERS, 2 * PX, CH), F32),
-            v((2 * PX, HEAD), F32),
+            v((ROWS, 2 * LANES), F32),
             v((2 * PX, HEAD), F32),
             v((2 * PX, MAIN), F32),
-            v((2 * PX, CH), F32),
+            v((PX, CH), F32),
             v((2, PX, CH), BF16),
             v((TILE, LAB + TGT), F32),
             v((TILE, LAB + TGT), F32),

time: 104 us -> 97.8 us (0.940)
  Pallas kernels: 103 us -> 97 us
    pallas_call x1, Pallas kernels: 101 us -> 94.5 us  [fast(): pl.pallas_call(head_kernel, out_shape=(out((tiles, 64, CH), BF16), out((2...]
where the time goes in v3:
time: 97.8 us; the launch traced here: 97.6 us
  Pallas kernels  97 us (99%)
    pallas_call x1, Pallas kernels, fast(): pl.pallas_call(head_kernel, out_shape=(out((tiles, 64, CH), BF16), out((2...  94.5 us
    pallas_call x1, Pallas kernels, fast(): pl.pallas_call(finish_kernel, out_shape=(out((tiles, 64, CH), BF16), out(...  2.44 us

profile of v3, /device:TPU:0, one launch (start us, length us, event | category | flops | bytes accessed | tf_op | source)
XLA Modules:
  0.0 97.6 jit_solution(13417407948796913507)
XLA Ops:
  0.6 94.5 %shard_map.241 = (bf16[4,64,256]{2,1,0:T(8,128)(2,1)}, f32[2,288,256]{2,1,0:T(8,128)}, f32[2,432,128]{2,1,0:T(8,128)}, f32[2,8,768]{2,1,0:T(8,128)}) custom-call(bf16[4,64,256]{2,1,0:T(8,128)(2,1)} %bitcast.7, f32[1,288,256]{2,1,0:T(8,128)} %tower_class.1, f32[1,288,256]{2,1,0:T(8,128)} %tower_boxes.1, f32[180,288]{1,0:T(8,128)} %bitcast.6, ...), custom_call_target="tpu_custom_call" | custom-call | tf_op jit(solution)/shard_map/pallas_call | solution.py:873
  95.2 2.4 %shard_map.242 = (bf16[4,64,256]{2,1,0:T(8,128)(2,1)}, f32[1,288,256]{2,1,0:T(8,128)}, f32[4,256]{1,0:T(4,128)}, f32[1,288,256]{2,1,0:T(8,128)}, f32[4,256]{1,0:...) custom-call(bf16[4,64,256]{2,1,0:T(8,128)(2,1)} %get-tuple-element.22.features, ...), custom_call_target="tpu_custom_call" | custom-call | tf_op jit(solution)/shard_map/pallas_call | solution.py:957

commit v4 on v3

--- a/solution.py
+++ b/solution.py
@@ -291,7 +291,7 @@
     "bT3", "bT2", "bU3", "aM1", "bU1", "aU2", "aM2", "cU0", "cT0", "y", "cT3", "cM0", "cT1", "cU3", "aM3", "cU1",
     "cT2", "bM1", "bU2", "F0", "bM2", "cU2", "bM3", "F1", "F2", "cM1", "dU3", "cM3", "cM2", "F3", "HM", "dU2",
     "dU0", "dU1", "WM0", "WM1", "HU", "X", "kM1", "kM0", "WU0", "w3", "x3", "kU0", "WU1", "k3", "w2", "kU1", "WU2",
-    "x2", "k2", "kU2", "w1", "x1", "p3", "kU3", "Bk", "p2", "k1", "w0", "WM2", "Bp", "q2", "k0", "x0", "p1", "rU0",
+    "x2", "k2", "kU2", "w1", "kU3", "x1", "p3", "Bk", "p2", "k1", "w0", "WM2", "Bp", "q2", "k0", "x0", "p1", "rU0",
     "q3", "kM3", "kM2", "Bq", "rU1", "rU2", "rU3", "q1", "pU0", "p0", "pM2", "pM0", "pM3", "s2", "q0", "pU3", "Bs",
     "pU1", "s3", "qU0", "pU2", "s1", "pM1", "D", "qM3", "qM0", "qM2", "s0", "qM1", "E", "qU3", "qU1", "qU2", "sM",
     "t", "sU",
@@ -299,9 +299,13 @@
 
 
 def head_kernel(
-    features, tower_class, tower_boxes, head_class, head_boxes, bias_class, bias_boxes, head_class_bias, head_boxes_bias,
-    state, labels, targets_in, valid, label, spread_any, targets_any, mask_lab_any, mask_tgt_any,
-    out_features, out_towers, out_heads, out_bias,
+    features_any, tower_class_any, tower_boxes_any, head_class_any, head_boxes_any,
+    bias_class_any, bias_boxes_any, head_class_bias_any, head_boxes_bias_any, state_any, labels_any, targets_in_any,
+    valid_any, label_any, spread_any, targets_any, mask_lab_any, mask_tgt_any,
+    to_features, to_towers, to_heads, to_bias,
+    out_features, out_towers, out_heads, out_bias, out_sem,
+    bias_class, bias_boxes, head_class_bias, head_boxes_bias, valid, label,
+    tower_class, tower_boxes, head_class, head_boxes, features, state, labels, targets_in,
     spread, targets, mask_lab, mask_tgt, bias, fetch_sem,
     own, own_h, own_v, w, wh, hp, hv, g, gh, rc, rch, sm, su, sv, r1a, r1b, r1m, r1u, r1v, r2, r2m, r2u, r2v,
     quarter, sum_m, sum_u, sum_v, rz, rzm, rzu, rzv, done, layer_in,
@@ -333,14 +337,23 @@
     for peer in peers:
         pl.semaphore_signal(barrier, inc=1, device_id=peer, device_id_type=MESH)
 
-    constants_in = [
+    fetched = [
         pltpu.make_async_copy(src, dst, fetch_sem.at[i])
         for i, (src, dst) in enumerate(
-            ((mask_lab_any, mask_lab), (spread_any.at[role], spread), (mask_tgt_any, mask_tgt), (targets_any, targets))
+            (
+                (tower_class_any, tower_class), (tower_boxes_any, tower_boxes), (head_class_any, head_class),
+                (head_boxes_any, head_boxes), (features_any, features), (state_any, state), (labels_any, labels),
+                (targets_in_any, targets_in), (valid_any, valid), (mask_lab_any, mask_lab),
+                (spread_any.at[role], spread), (mask_tgt_any, mask_tgt), (targets_any, targets), (label_any, label),
+                (bias_class_any, bias_class), (bias_boxes_any, bias_boxes),
+                (head_class_bias_any, head_class_bias), (head_boxes_bias_any, head_boxes_bias),
+            )
         )
     ]
-    for copy in constants_in:
+    for copy in fetched:
         copy.start()
+    for copy in fetched[:4]:
+        copy.wait()
 
     own[0] = tower_class[0].astype(BF16)
     own[1] = tower_boxes[0].astype(BF16)
@@ -352,21 +365,6 @@
     own_h[ROWS:PACK, :] = (spare[0:HALF, 0:LANES] + pltpu.roll(spare[HALF:ROWS, 0:LANES], TAIL, 1)).astype(BF16)
     own_v[...] = folded(spare[:, LANES : 2 * LANES]).astype(BF16)
 
-    row = lax.broadcasted_iota(jnp.int32, (TILE, TILE * A), 0)
-    found = jnp.zeros((TILE, TILE * A), F32)
-    for t in range(SECTIONS):
-        found += jnp.where(jnp.logical_and(state[t] == 1, row < valid[t]), 1.0, 0.0)
-    count_mine[...] = jnp.full((8, LANES), jnp.sum(found), F32)
-    inside = row < valid[s]
-    kind = state[s]
-    lab[...] = jnp.zeros_like(lab)
-    lab[:, 0 : TILE * A] = jnp.where(
-        inside,
-        jnp.where(kind == 1, labels[s].astype(F32) + 2.0, jnp.where(kind == 2, 0.0, 1.0)),
-        0.0,
-    )
-    lab[:, LAB : LAB + targets_in.shape[2]] = targets_in[s]
-
     pl.semaphore_wait(barrier, len(peers))
 
     def kinds(kind_name):
@@ -407,6 +405,22 @@
         return pl.ds(pl.multiple_of(64 * sec, 64), 64)
 
     def features_send():
+        for copy in fetched[4:9]:
+            copy.wait()
+        row = lax.broadcasted_iota(jnp.int32, (TILE, TILE * A), 0)
+        found = jnp.zeros((TILE, TILE * A), F32)
+        for t in range(SECTIONS):
+            found += jnp.where(jnp.logical_and(state[t] == 1, row < valid[t]), 1.0, 0.0)
+        count_mine[...] = jnp.full((8, LANES), jnp.sum(found), F32)
+        inside = row < valid[s]
+        kind = state[s]
+        lab[...] = jnp.zeros_like(lab)
+        lab[:, 0 : TILE * A] = jnp.where(
+            inside,
+            jnp.where(kind == 1, labels[s].astype(F32) + 2.0, jnp.where(kind == 2, 0.0, 1.0)),
+            0.0,
+        )
+        lab[:, LAB : LAB + targets_in.shape[2]] = targets_in[s]
         for name, peer, sec in in_plane:
             net.send(("f", name), features.at[sec], x.at[0, rows_of(s), :], peer)
         net.send("count c", count_mine, count_in.at[0], to_c)
@@ -509,7 +523,7 @@
                 ref[t, 0:TILE, :] = jnp.zeros((TILE, ref.shape[2]), BF16)
                 ref[t, TILE + PX : 2 * TILE + PX, :] = jnp.zeros((TILE, ref.shape[2]), BF16)
         grad_bias[...] = jnp.zeros_like(grad_bias)
-        for copy in constants_in:
+        for copy in fetched[9:]:
             copy.wait()
         bias[0:LAYERS, 0:CH] = jnp.where(role == 0, bias_class[...], bias_boxes[...])
         bias[4:5, :] = jnp.where(role == 0, lay(head_class_bias[...]), lay(head_boxes_bias[...]))
@@ -617,6 +631,7 @@
             net.arrived("layer", layer_in.at[sec], peer, span=SECTIONS, offset=sec)
             for i in range(2):
                 out_towers[i, half_rows(sec // 2), half_lanes(sec % 2)] = layer_in[sec, i].astype(F32)
+        give(out_towers, to_towers)
 
     def head_refs(kind):
         return dict(
@@ -726,6 +741,8 @@
 
         if kind_name == "U":
             out_heads[1, ROWS:PACK] = jnp.zeros((HALF, LANES), F32)
+        rows = pl.ds(0, ROWS) if kind_name == "M" else pl.ds(ROWS, HALF)
+        give(out_heads.at[:, rows], to_heads.at[:, rows])
 
     def bias_cores():
         net.arrived("bias c", bias_in.at[0], to_c)
@@ -748,6 +765,14 @@
             net.arrived(("bias z", k), bias_in.at[2 + k], to_z(PLANES - k))
         out_bias[role] = bias_z[2] + bias_in[4]
         out_bias[1 - role] = bias_in[3] + bias_in[5]
+        give(out_bias, to_bias)
+
+    results = []
+
+    def give(src, dst):
+        copy = pltpu.make_async_copy(src, dst, out_sem.at[len(results)])
+        copy.start()
+        results.append(copy)
 
     def features_sum():
         net.arrived("dx", dx_in, to_pair)
@@ -760,6 +785,7 @@
             net.arrived(("b", name), features_in.at[sec], peer)
             out_features[sec] = features_in[sec]
         out_features[s] = tile_out[rows_of(s), :]
+        give(out_features, to_features)
 
     def head_gradient(kind_name, r):
         if kind_name == "M":
@@ -805,6 +831,8 @@
     )
     for step in SCHEDULE:
         steps[step[0]](*(int(v) if v.isdigit() else v for v in step[1:]))
+    for copy in results:
+        copy.wait()
     net.finish()
 
 
@@ -866,7 +894,6 @@
     spread, targets, mask_lab, mask_tgt, label = constants(class_width, boxes_width)
     tiles = features.shape[0]
     vmem = pl.BlockSpec(memory_space=pltpu.VMEM)
-    smem = pl.BlockSpec(memory_space=pltpu.SMEM)
     v = lambda shape, dtype: pltpu.VMEM(shape, dtype)
     out = lambda shape, dtype: jax.ShapeDtypeStruct(shape, dtype)
     anywhere = pl.BlockSpec(memory_space=pl.ANY)
@@ -878,15 +905,34 @@
             out((2, PACK, LANES), F32),
             out((2, 8, HEAD), F32),
         ),
-        in_specs=[vmem] * 12 + [smem, vmem] + [anywhere] * 4,
-        out_specs=(vmem,) * 4,
+        in_specs=[anywhere] * 18,
+        out_specs=(anywhere,) * 4,
         scratch_shapes=[
+            v((tiles, 64, CH), BF16),
+            v((2, ROWS, CH), F32),
+            v((2, PACK, LANES), F32),
+            v((2, 8, HEAD), F32),
+            pltpu.SemaphoreType.DMA((5,)),
+            v(bias_class.shape, F32),
+            v(bias_boxes.shape, F32),
+            v(head_class_bias.shape, F32),
+            v(head_boxes_bias.shape, F32),
+            pltpu.SMEM(valid_rows.shape, jnp.int32),
+            v(label.shape, F32),
+            v(tower_class.shape, F32),
+            v(tower_boxes.shape, F32),
+            v(head_class.shape[::-1], F32),
+            v(head_boxes.shape[::-1], F32),
+            v((tiles, 64, CH), BF16),
+            v(anchor_state.shape, jnp.int32),
+            v(class_labels.shape, jnp.int32),
+            v(box_targets.shape, F32),
             v(spread.shape[1:], BF16),
             v(targets.shape, BF16),
             v(mask_lab.shape, BF16),
             v(mask_tgt.shape, BF16),
             v((8, HEAD), F32),
-            pltpu.SemaphoreType.DMA((4,)),
+            pltpu.SemaphoreType.DMA((18,)),
             v((2, ROWS, CH), BF16),
             v((PACK, LANES), BF16),
             v((FOLD_ROWS, LANES), BF16),

time: 97.8 us -> 96.6 us (0.988)
  Pallas kernels: 97 us -> 95.7 us
    pallas_call x1, Pallas kernels: 94.5 us -> 93.3 us  [fast(): pl.pallas_call(head_kernel, out_shape=(out((tiles, 64, CH), BF16), out((2...]
where the time goes in v4:
time: 96.6 us; the launch traced here: 96.4 us
  Pallas kernels  95.7 us (99%)
    pallas_call x1, Pallas kernels, fast(): pl.pallas_call(head_kernel, out_shape=(out((tiles, 64, CH), BF16), out((2...  93.3 us
    pallas_call x1, Pallas kernels, fast(): pl.pallas_call(finish_kernel, out_shape=(out((tiles, 64, CH), BF16), out(...  2.44 us

profile of v4, /device:TPU:0, one launch (start us, length us, event | category | flops | bytes accessed | tf_op | source)
XLA Modules:
  0.0 96.4 jit_solution(8201909371129097132)
XLA Ops:
  0.6 93.3 %shard_map.241 = (bf16[4,64,256]{2,1,0:T(8,128)(2,1)}, f32[2,288,256]{2,1,0:T(8,128)}, f32[2,432,128]{2,1,0:T(8,128)}, f32[2,8,768]{2,1,0:T(8,128)}) custom-call(bf16[4,64,256]{2,1,0:T(8,128)(2,1)} %bitcast.7, f32[1,288,256]{2,1,0:T(8,128)} %tower_class_any.1, f32[1,288,256]{2,1,0:T(8,128)} %tower_boxes_any.1, f32[180,288]{1,0:T(8,128)} %bitcast.6, ...), custom_call_target="tpu_custom_call" | custom-call | tf_op jit(solution)/shard_map/pallas_call | solution.py:900
  93.9 2.4 %shard_map.242 = (bf16[4,64,256]{2,1,0:T(8,128)(2,1)}, f32[1,288,256]{2,1,0:T(8,128)}, f32[4,256]{1,0:T(4,128)}, f32[1,288,256]{2,1,0:T(8,128)}, f32[4,256]{1,0:...) custom-call(bf16[4,64,256]{2,1,0:T(8,128)(2,1)} %get-tuple-element.22.features, ...), custom_call_target="tpu_custom_call" | custom-call | tf_op jit(solution)/shard_map/pallas_call | solution.py:1003

commit v5 on v4

--- a/solution.py
+++ b/solution.py
@@ -287,14 +287,7 @@
     "T0": "A", "T1": "B", "T3": "A", "T2": "B", "M0": "B", "M1": "A", "M3": "B", "M2": "A", "U0": "A", "U1": "B", "U3": "A", "U2": "B",
 }
 SCHEDULE = (
-    "zT", "aM0", "aT0", "aU0", "aT1", "bT0", "f", "aT3", "bT1", "bM0", "zU", "aT2", "zM", "bU0", "e", "aU1", "aU3",
-    "bT3", "bT2", "bU3", "aM1", "bU1", "aU2", "aM2", "cU0", "cT0", "y", "cT3", "cM0", "cT1", "cU3", "aM3", "cU1",
-    "cT2", "bM1", "bU2", "F0", "bM2", "cU2", "bM3", "F1", "F2", "cM1", "dU3", "cM3", "cM2", "F3", "HM", "dU2",
-    "dU0", "dU1", "WM0", "WM1", "HU", "X", "kM1", "kM0", "WU0", "w3", "x3", "kU0", "WU1", "k3", "w2", "kU1", "WU2",
-    "x2", "k2", "kU2", "w1", "kU3", "x1", "p3", "Bk", "p2", "k1", "w0", "WM2", "Bp", "q2", "k0", "x0", "p1", "rU0",
-    "q3", "kM3", "kM2", "Bq", "rU1", "rU2", "rU3", "q1", "pU0", "p0", "pM2", "pM0", "pM3", "s2", "q0", "pU3", "Bs",
-    "pU1", "s3", "qU0", "pU2", "s1", "pM1", "D", "qM3", "qM0", "qM2", "s0", "qM1", "E", "qU3", "qU1", "qU2", "sM",
-    "t", "sU",
+    "zT", "aM0", "aT0", "aU0", "aT1", "bT0", "f", "aT3", "bT1", "bM0", "zU", "aT2", "zM", "bU0", "e", "aU1", "aU3", "bT3", "bT2", "bU3", "aM1", "bU1", "aU2", "aM2", "cU0", "cT0", "y", "cT3", "cM0", "cT1", "cU3", "aM3", "cU1", "cT2", "bM1", "bU2", "F0", "bM2", "cU2", "bM3", "F1", "F2", "cM1", "dU3", "cM3", "cM2", "F3", "HM", "dU2", "dU0", "dU1", "WM0", "WM1", "HU", "X", "kM1", "kM0", "WU0", "w3", "x3", "kU0", "WU1", "k3", "w2", "kU1", "WU2", "x2", "k2", "kU2", "w1", "kU3", "x1", "p3", "Bk", "p2", "k1", "w0", "WM2", "Bp", "q2", "k0", "kM2", "kM3", "x0", "p1", "rU0", "q3", "Bq", "rU1", "rU2", "rU3", "q1", "pU0", "p0", "pM2", "pM0", "pM3", "s2", "q0", "pU3", "Bs", "pU1", "s3", "qU0", "pU2", "s1", "pM1", "D", "qM3", "qM0", "qM2", "s0", "qM1", "E", "qU3", "qU1", "qU2", "sM", "t", "sU",
 )
 
 

time: 96.6 us -> 98.4 us (1.019)
  Pallas kernels: 95.7 us -> 97.6 us
    pallas_call x1, Pallas kernels: 93.3 us -> 95.2 us  [fast(): pl.pallas_call(head_kernel, out_shape=(out((tiles, 64, CH), BF16), out((2...]
where the time goes in v5:
time: 98.4 us; the launch traced here: 98.3 us
  Pallas kernels  97.6 us (99%)
    pallas_call x1, Pallas kernels, fast(): pl.pallas_call(head_kernel, out_shape=(out((tiles, 64, CH), BF16), out((2...  95.2 us
    pallas_call x1, Pallas kernels, fast(): pl.pallas_call(finish_kernel, out_shape=(out((tiles, 64, CH), BF16), out(...  2.44 us

profile of v5, /device:TPU:0, one launch (start us, length us, event | category | flops | bytes accessed | tf_op | source)
XLA Modules:
  0.0 98.3 jit_solution(4844932050342734071)
XLA Ops:
  0.6 95.2 %shard_map.241 = (bf16[4,64,256]{2,1,0:T(8,128)(2,1)}, f32[2,288,256]{2,1,0:T(8,128)}, f32[2,432,128]{2,1,0:T(8,128)}, f32[2,8,768]{2,1,0:T(8,128)}) custom-call(bf16[4,64,256]{2,1,0:T(8,128)(2,1)} %bitcast.7, f32[1,288,256]{2,1,0:T(8,128)} %tower_class_any.1, f32[1,288,256]{2,1,0:T(8,128)} %tower_boxes_any.1, f32[180,288]{1,0:T(8,128)} %bitcast.6, ...), custom_call_target="tpu_custom_call" | custom-call | tf_op jit(solution)/shard_map/pallas_call | solution.py:893
  95.8 2.4 %shard_map.242 = (bf16[4,64,256]{2,1,0:T(8,128)(2,1)}, f32[1,288,256]{2,1,0:T(8,128)}, f32[4,256]{1,0:T(4,128)}, f32[1,288,256]{2,1,0:T(8,128)}, f32[4,256]{1,0:...) custom-call(bf16[4,64,256]{2,1,0:T(8,128)(2,1)} %get-tuple-element.22.features, ...), custom_call_target="tpu_custom_call" | custom-call | tf_op jit(solution)/shard_map/pallas_call | solution.py:996
